TPU v7x, 256 devices: a whole 4x4x8 slice. The times are simulated.
256 devices in a mesh: mem: 16 (over y_lo, x, core), tile: 16 (over y_hi, z).
Axes of the slice: x: 4, y: 4 (y_hi: 2, y_lo: 2; y = y_hi * 2 + y_lo), z: 8, core: 2. Of those that a mesh axis runs over, the one named last changes fastest.
Arguments:
- perturb: bfloat16 [80, 2, 2, 256, 2048], P('mem', None, None, None, 'tile'), may hold values from -6 to 6
- coef_x: float32 [2, 256, 2048], P(None, None, 'tile'), may hold values from 0.25 to 0.5
- coef_y: float32 [2, 256, 2048], P(None, None, 'tile'), may hold values from 0.25 to 0.5
- obs_values: float32 [524288], P(('mem', 'tile')), may hold values from -12 to 12
- obs_tile: int32 [524288, 1], P(('mem', 'tile')), may hold values from 0 to 15; in each aligned block of 2048 rows (0 to 2047, 2048 to 4095, ...) at most 384 rows name the same one
- obs_cell: int32 [524288], P(('mem', 'tile')), may hold values from 0 to 131071
Outputs:
- increment: float32 [256, 2, 2, 2048], P('mem', None, None, 'tile')
Inputs may be any that keep to these rules, and one draw needn't show every extreme that they name: `obs_tile`: among the 2048 observations of one device no tile is named more than 384 times, and in every draw some device names some tile exactly 384 times.
All inputs are finite; a program needn't handle non-finite values.
Results may differ from a plain program's by a relative error of at most 0.0003.
Values sent between devices are 32-bit elements; how exact they have to be, the bound alone decides.
A program may use at most 64 MiB of HBM per device.

v0:
```python
import jax
import jax.numpy as jnp
from jax import lax
from jax.sharding import PartitionSpec as P

FIELDS = 2
LEVELS = 2
SWEEPS = 6
LAT = 256


def extended_2(block, sides, width):
    for axis, dim in sides:
        count = lax.axis_size(axis)
        forward = [(i, i + 1) for i in range(count - 1)]
        forward.append((count - 1, 0))
        backward = [(target, source) for source, target in forward]
        low = lax.ppermute(
            lax.slice_in_dim(block, block.shape[dim] - width, None, axis=dim), axis, forward
        )
        high = lax.ppermute(lax.slice_in_dim(block, 0, width, axis=dim), axis, backward)
        block = jnp.concatenate([low, block, high], axis=dim)
    return block


def sweep_east(field, coef):
    flux = coef[..., :-1] * (field[..., 1:] - field[..., :-1])
    return field[..., 1:-1] + flux[..., 1:] - flux[..., :-1]


def sweep_north(field, coef):
    flux = coef[..., :-1, :] * (field[..., 1:, :] - field[..., :-1, :])
    zero_row = jnp.zeros(field.shape[:-2] + (1, field.shape[-1]), jnp.float32)
    upper = jnp.concatenate([flux, zero_row], axis=-2)
    lower = jnp.concatenate([zero_row, flux], axis=-2)
    return field + upper - lower


def deposit(lists, total_cells):
    cells = lists[1].astype(jnp.int32)
    return jnp.zeros((total_cells,), jnp.float32).at[cells].add(lists[0])


def on_device(perturb, coef_x, coef_y, obs_values, obs_tile, obs_cell):
    tiles = lax.axis_size("tile")
    members = perturb.shape[0] * lax.axis_size("mem")
    lon_local = perturb.shape[4]
    capacity = 3 * obs_values.shape[0] // tiles
    total_cells = FIELDS * LEVELS * LAT * lon_local
    target = obs_tile[:, 0]
    onehot = (jnp.arange(tiles, dtype=jnp.int32)[:, None] == target[None, :]).astype(jnp.int32)
    before = jnp.cumsum(onehot, axis=1) - onehot
    ranking = jnp.sum(before * onehot, axis=0)
    slot = target * capacity + ranking
    packed = jnp.stack([obs_values, obs_cell.astype(jnp.float32)])
    outgoing = jnp.zeros((2, tiles * capacity), jnp.float32).at[:, slot].set(packed)
    incoming = lax.all_to_all(outgoing, "tile", split_axis=1, concat_axis=1, tiled=True)
    adjoint_field = lax.psum(deposit(incoming, total_cells), "mem")
    adjoint_field = adjoint_field.reshape(FIELDS, LEVELS, LAT, lon_local)
    widened = perturb.astype(jnp.float32)
    product = jnp.sum(widened * adjoint_field[None], axis=1)
    joined = jnp.concatenate([product, coef_x[None]], axis=0)
    padded = extended_2(joined, (("tile", 3),), 1)
    coef_wide = padded[-1]
    product = sweep_east(padded[:-1], coef_wide)
    for step in range(SWEEPS - 1):
        extended = extended_2(product, (("tile", 3),), 1)
        product = sweep_east(extended, coef_wide)
    for step in range(SWEEPS):
        product = sweep_north(product, coef_y)
    summed = lax.psum_scatter(
        jnp.einsum("kflyx,klyx->yflx", widened, product), "mem", scatter_dimension=0, tiled=True
    )
    return summed / (members - 1)


def solution(mesh):
    return jax.shard_map(
        on_device,
        mesh=mesh,
        in_specs=(
            P("mem", None, None, None, "tile"),
            P(None, None, "tile"),
            P(None, None, "tile"),
            P(("mem", "tile")),
            P(("mem", "tile"), None),
            P(("mem", "tile")),
        ),
        out_specs=P("mem", None, None, "tile"),
        check_vma=False,
    )
```

profile of v0, /device:TPU:1, one launch (start us, length us, event | category | flops | bytes accessed | tf_op | source)
XLA Modules:
  0.0 436.7 jit_solution(9558857455044095042)
XLA Ops:
  7.2 4.5 %reduce-window.6 = s32[16,16,128]{2,1,0:T(8,128)S(1)} reduce-window(s32[16,16,128]{2,1,0:T(8,128)S(1)} %fusion.18, s32[]{:T(128)} %constant.8.clone.1), window={size=1x1x128 pad=0_0x0_0x127_0}, to_apply=%region_0.0 | reduce-window | flops 4161536 | bytes 262148 | tf_op jit(solution)/shard_map/reduce-window
  16.7 6.7 %scatter_custom_fusion = f32[2,6144]{0,1:T(8,128)S(1)} fusion(s32[2048]{0:T(1024)S(1)} %bitcast.52, f32[2048,2]{1,0:T(8,128)} %copy.13, f32[]{:T(128)} %constant.6.clone.1), kind=kCustom, calls=%fused_computation.22 | custom fusion | bytes 49664 | tf_op jit(solution)/shard_map/scatter | solution.py:56
  24.6 20.4 %all_to_all.9 = f32[2,16,384]{2,0,1:T(2,128)S(1)} all-to-all(f32[2,16,384]{2,0,1:T(2,128)S(1)} %copy.14), channel_id=1, replica_groups=mesh['mem'=16,'tile'=16] {'tile'}, dimensions={1} | all-to-all | bytes 98304 | tf_op jit(solution)/shard_map/all_to_all | solution.py:57
  45.1 41.6 %scatter_custom_fusion.1 = f32[131072]{0:T(1024)} fusion(s32[6144]{0:T(1024)S(1)} %bitcast.50, f32[6144]{0:T(1024)S(1)} %bitcast.51, f32[]{:T(128)} %constant.6.clone.1), kind=kCustom, calls=%fused_computation.59 | custom fusion | flops 6144 | bytes 524292 | tf_op jit(solution)/shard_map/scatter-add | solution.py:41
  86.8 119.1 %all-reduce.16.cloned.1.call-done = f32[2,2,256,128]{3,2,1,0:T(8,128)} async-done(((f32[2,2,256,128]{3,2,1,0:T(8,128)}), f32[2,2,256,128]{3,2,1,0:T(8,128)}) %all-reduce.16.cloned.1.call-update) | async-done | bytes 524304 | tf_op jit(solution)/shard_map/psum | solution.py:58
  205.8 1.9 multiply_reduce_fusion.1
  207.7 2.2 pad_maximum_fusion.4
  209.9 1.9 copy.15
  213.1 1.9 copy.16
  215.0 4.0 collective-permute-start.1
  218.9 1.7 copy.17
  220.6 1.7 copy.18
  227.0 1.7 copy.21
  228.7 4.5 %collective-permute-start.2 = (f32[5,2,256,1]{2,1,3,0:T(2,128)S(1)}, f32[5,2,256,1]{2,1,3,0:T(2,128)S(1)}, u32[]{:S(2)}, u32[]{:S(2)}) collective-permute-start(f32[5,2,256,1]{2,1,3,0:T(2,128)S(1)} %copy.21), channel_id=1, source_target_pairs={{1,0},{2,1},{3,2},{4,3},{5,4},{6,5},{7,6},{8,7},{9,8},{10,9},{11,1... | collective-permute-start | bytes 30728 | tf_op jit(solution)/shard_map/ppermute | solution.py:21
  234.5 5.5 %collective-permute-done.3 = f32[5,2,256,1]{2,1,3,0:T(2,128)S(1)} collective-permute-done((f32[5,2,256,1]{2,1,3,0:T(2,128)S(1)}, f32[5,2,256,1]{2,1,3,0:T(2,128)S(1)}, u32[]{:S(2)}, u32[]{:S(2)}) %collective-permute-start.3) | collective-permute-done | bytes 10272 | tf_op jit(solution)/shard_map/ppermute | solution.py:18
  240.0 1.5 copy.24
  241.5 2.1 fusion.2
  245.5 1.7 copy.25
  250.2 3.6 collective-permute-done.5
  253.8 1.5 copy.28
  255.3 2.1 fusion.3
  259.3 1.7 copy.29
  264.0 3.6 collective-permute-done.7
  269.2 2.1 fusion.4
  273.1 1.7 copy.33
  275.3 1.7 collective-permute-start.9
  277.9 3.8 collective-permute-done.9
  283.2 2.1 fusion.5
  287.2 1.7 copy.37
  291.9 3.6 collective-permute-done.11
  297.1 2.1 fusion.6
  306.2 122.3 %all-reduce.18.cloned.1.call-done = f32[256,2,2,128]{3,2,1,0:T(2,128)} async-done(((f32[256,2,2,128]{3,2,1,0:T(2,128)}), f32[256,2,2,128]{3,2,1,0:T(2,128)}) %all-reduce.18.cloned.1.call-update) | async-done | bytes 524304
  (85 shorter events, 44.3 us)
Async XLA Ops:
  6.5 199.3 %all-reduce.16.cloned.1.call-start = ((), (), s32[]{:S(2)}) async-start(), calls=%async_computation.1 | async-start | bytes 1048576 | tf_op jit(solution)/shard_map/psum | solution.py:58
  86.7 121.0 %copy-start.4 = (f32[2,256,128]{2,1,0:T(8,128)S(1)}, f32[2,256,128]{2,1,0:T(8,128)}, u32[]{:S(2)}) copy-start(f32[2,256,128]{2,1,0:T(8,128)} %param.7) | copy-start | bytes 786436
  86.7 341.8 %all-reduce.18.cloned.1.call-start = ((), (), s32[]{:S(2)}) async-start(), calls=%async_computation.2 | async-start | bytes 1048576
  211.8 7.2 %collective-permute-start = (f32[6,2,256,1]{2,1,3,0:T(2,128)S(1)}, f32[6,2,256,1]{2,1,3,0:T(2,128)S(1)}, u32[]{:S(2)}, u32[]{:S(2)}) collective-permute-start(f32[6,2,256,1]{2,1,3,0:T(2,128)S(1)} %copy.15), channel_id=1, source_target_pairs={{0,1},{1,2},{2,3},{3,4},{4,5},{5,6},{6,7},{7,8},{8,9},{9,10},{10,1... | collective-permute-start | bytes 36872 | tf_op jit(solution)/shard_map/ppermute | solution.py:18
  215.0 5.7 %collective-permute-start.1 = (f32[6,2,256,1]{2,1,3,0:T(2,128)S(1)}, f32[6,2,256,1]{2,1,3,0:T(2,128)S(1)}, u32[]{:S(2)}, u32[]{:S(2)}) collective-permute-start(f32[6,2,256,1]{2,1,3,0:T(2,128)S(1)} %copy.16), channel_id=1, source_target_pairs={{1,0},{2,1},{3,2},{4,3},{5,4},{6,5},{7,6},{8,7},{9,8},{10,9},{11,1... | collective-permute-start | bytes 36872 | tf_op jit(solution)/shard_map/ppermute | solution.py:21
  222.3 1.6 copy-start
  222.3 2.0 copy-start.1
  228.7 5.3 %collective-permute-start.2 = (f32[5,2,256,1]{2,1,3,0:T(2,128)S(1)}, f32[5,2,256,1]{2,1,3,0:T(2,128)S(1)}, u32[]{:S(2)}, u32[]{:S(2)}) collective-permute-start(f32[5,2,256,1]{2,1,3,0:T(2,128)S(1)} %copy.21), channel_id=1, source_target_pairs={{1,0},{2,1},{3,2},{4,3},{5,4},{6,5},{7,6},{8,7},{9,8},{10,9},{11,1... | collective-permute-start | bytes 30728 | tf_op jit(solution)/shard_map/ppermute | solution.py:21
  233.6 6.4 %collective-permute-start.3 = (f32[5,2,256,1]{2,1,3,0:T(2,128)S(1)}, f32[5,2,256,1]{2,1,3,0:T(2,128)S(1)}, u32[]{:S(2)}, u32[]{:S(2)}) collective-permute-start(f32[5,2,256,1]{2,1,3,0:T(2,128)S(1)} %copy.23), channel_id=1, source_target_pairs={{0,1},{1,2},{2,3},{3,4},{4,5},{5,6},{6,7},{7,8},{8,9},{9,10},{10,1... | collective-permute-start | bytes 30728 | tf_op jit(solution)/shard_map/ppermute | solution.py:18
  247.2 2.6 collective-permute-start.4
  247.6 6.2 %collective-permute-start.5 = (f32[5,2,256,1]{2,1,3,0:T(2,128)S(1)}, f32[5,2,256,1]{2,1,3,0:T(2,128)S(1)}, u32[]{:S(2)}, u32[]{:S(2)}) collective-permute-start(f32[5,2,256,1]{2,1,3,0:T(2,128)S(1)} %copy.27), channel_id=1, source_target_pairs={{0,1},{1,2},{2,3},{3,4},{4,5},{5,6},{6,7},{7,8},{8,9},{9,10},{10,1... | collective-permute-start | bytes 30728 | tf_op jit(solution)/shard_map/ppermute | solution.py:18
  261.0 2.6 collective-permute-start.6
  261.5 6.2 %collective-permute-start.7 = (f32[5,2,256,1]{2,1,3,0:T(2,128)S(1)}, f32[5,2,256,1]{2,1,3,0:T(2,128)S(1)}, u32[]{:S(2)}, u32[]{:S(2)}) collective-permute-start(f32[5,2,256,1]{2,1,3,0:T(2,128)S(1)} %copy.31), channel_id=1, source_target_pairs={{0,1},{1,2},{2,3},{3,4},{4,5},{5,6},{6,7},{7,8},{8,9},{9,10},{10,1... | collective-permute-start | bytes 30728 | tf_op jit(solution)/shard_map/ppermute | solution.py:18
  274.9 2.6 collective-permute-start.8
  275.3 6.4 %collective-permute-start.9 = (f32[5,2,256,1]{2,1,3,0:T(2,128)S(1)}, f32[5,2,256,1]{2,1,3,0:T(2,128)S(1)}, u32[]{:S(2)}, u32[]{:S(2)}) collective-permute-start(f32[5,2,256,1]{2,1,3,0:T(2,128)S(1)} %copy.35), channel_id=1, source_target_pairs={{0,1},{1,2},{2,3},{3,4},{4,5},{5,6},{6,7},{7,8},{8,9},{9,10},{10,1... | collective-permute-start | bytes 30728 | tf_op jit(solution)/shard_map/ppermute | solution.py:18
  288.9 2.6 collective-permute-start.10
  289.4 6.2 %collective-permute-start.11 = (f32[5,2,256,1]{2,1,3,0:T(2,128)S(1)}, f32[5,2,256,1]{2,1,3,0:T(2,128)S(1)}, u32[]{:S(2)}, u32[]{:S(2)}) collective-permute-start(f32[5,2,256,1]{2,1,3,0:T(2,128)S(1)} %copy.39), channel_id=1, source_target_pairs={{0,1},{1,2},{2,3},{3,4},{4,5},{5,6},{6,7},{7,8},{8,9},{9,10},{10,1... | collective-permute-start | bytes 30728 | tf_op jit(solution)/shard_map/ppermute | solution.py:18
  299.1 1.0 copy-start.2
  302.1 1.3 copy-start.3
  303.7 1.2 copy-start.5
Sparse Core Ops, SparseCore 0:
  86.8 118.9 all-reduce.15
  305.1 123.3 all-reduce.17
where the time goes:
time: 437 us
  waiting for transfers between devices  264 us (60%)
  other arithmetic  72.8 us (17%)
  local copies, waits for them, and re-layouts  48.6 us (11%)
  blocking collectives  20.4 us (5%)
  starting transfers between devices  16.5 us (4%)
  between operations  14.4 us (3%)
    unnamed x3, waiting for transfers between devices  122 us
    psum x1, waiting for transfers between devices, on_device(): adjoint_field = lax.psum(deposit(incoming, total_cells), 'mem')  119 us
    scatter-add x1, other arithmetic, deposit(): return jnp.zeros((total_cells,), jnp.float32).at[cells].add(lists[0])  41.6 us
    all_to_all x1, blocking collectives, on_device(): lax.all_to_all(outgoing, 'tile', split_axis=1, concat_axis=1, tiled=True)  20.4 us
    ppermute x6, waiting for transfers between devices, extended_2(): lax.ppermute(lax.slice_in_dim(block, block.shape[dim] - width, None, axis...  20.2 us
    slice x11, local copies, waits for them, and re-layouts, extended_2(): lax.slice_in_dim(block, block.shape[dim] - width, None, axis=dim)  11.4 us
    mul x6, other arithmetic, sweep_east(): flux = coef[..., :-1] * (field[..., 1:] - field[..., :-1])  11 us
    slice x6, local copies, waits for them, and re-layouts, extended_2(): lax.slice_in_dim(block, 0, width, axis=dim)  10.4 us
  transfers between devices with their start and end apart: 14, of which 12 were waited for; matrix products, arithmetic and copies ran while one was open for 2% of the time, Pallas kernels for 0%

commit v1 on v0

v1 whole, which is shorter than its diff:
```python
import functools

import jax
import jax.numpy as jnp
from jax import lax
from jax.experimental import pallas as pl
from jax.experimental.pallas import tpu as pltpu
from jax.sharding import PartitionSpec as P

FIELDS = 2
LEVELS = 2
SWEEPS = 6
LAT = 256
LON = 128
CAP = 384
LANES = 128
GROUPS = LAT // 8
BLOCKS = FIELDS * LEVELS * GROUPS
F32 = jnp.float32
BF16 = jnp.bfloat16
I32 = jnp.int32
NT = (((1,), (1,)), ((), ()))
NN = (((1,), (0,)), ((), ()))


def iota(shape, dim):
    return lax.broadcasted_iota(I32, shape, dim)


def dot(a, b, dims):
    return lax.dot_general(a, b, dims, preferred_element_type=F32)


def split(x):
    high = x.astype(BF16).astype(F32)
    return high, x - high


def pack_edges(load):
    lane = iota((8, LANES), 1)
    packed = jnp.zeros((8, LANES), F32)
    for g in range(8):
        place = (lane >= 16 * g) & (lane < 16 * g + 2 * SWEEPS)
        packed = jnp.where(place, pltpu.roll(load(g), SWEEPS + 16 * g, 1), packed)
    return packed


def merge_edges(west, east):
    return jnp.where(iota((8, LANES), 1) % 16 < SWEEPS, west, east)


def unpack_edges(merged, store):
    lane = iota((8, LANES), 1)
    halo = (lane < SWEEPS) | (lane >= LANES - SWEEPS)
    for g in range(8):
        store(g, jnp.where(halo, pltpu.roll(merged, LANES - SWEEPS - 16 * g, 1), 0.0))


def kernel(
    perturb_hbm, coef_x_hbm, coef_y_hbm, values_ref, tile_ref, cell_ref, out_ref,
    perturb_raw, coef_x_raw, coef_y_raw, perturb, perturb_halo, coef_x, coef_x_halo, coef_y,
    lists_out, lists_in, columns, total, partial, partial_in, adjoint, adjoint_halo,
    edges_out, edges_in, own_edges, near_edges, all_edges, product, terms, terms_in,
    load_sem, list_send, list_recv, edge_send, edge_recv, part_send, part_recv,
    adj_send, adj_recv, own_send, own_recv, all_send, all_recv, term_send, term_recv,
    *, mems, tiles, members,
):
    me_m, me_t = lax.axis_index("mem"), lax.axis_index("tile")
    west, east = lax.rem(me_t + tiles - 1, tiles), lax.rem(me_t + 1, tiles)
    blocks = values_ref.shape[0]
    slice_vecs = BLOCKS // mems

    def remote(src, dst, send, recv, m, t):
        return pltpu.make_async_remote_copy(
            src_ref=src, dst_ref=dst, send_sem=send, recv_sem=recv,
            device_id={"mem": m, "tile": t}, device_id_type=pl.DeviceIdType.MESH,
        )

    def other_m(d):
        return lax.rem(me_m + d, mems)

    def other_t(d):
        return lax.rem(me_t + d, tiles)

    loads = [
        pltpu.make_async_copy(src, dst, load_sem.at[i])
        for i, (src, dst) in enumerate(
            ((perturb_hbm, perturb_raw), (coef_x_hbm, coef_x_raw), (coef_y_hbm, coef_y_raw))
        )
    ]
    for copy in loads:
        copy.start()

    barrier = pltpu.get_barrier_semaphore()

    @pl.loop(1, mems)
    def _(d):
        pl.semaphore_signal(barrier, 1, device_id={"mem": other_m(d), "tile": me_t}, device_id_type=pl.DeviceIdType.MESH)

    @pl.loop(1, tiles)
    def _(d):
        pl.semaphore_signal(barrier, 1, device_id={"mem": me_m, "tile": other_t(d)}, device_id_type=pl.DeviceIdType.MESH)

    with jax.named_scope("bucket"):
        tile = tile_ref[...]
        hot = jnp.concatenate([jnp.where(tile == t, 1.0, 0.0) for t in range(tiles)], axis=0)
        hot16 = hot.astype(BF16)
        lane_r, lane_c = iota((LANES, 2 * LANES), 0), iota((LANES, 2 * LANES), 1)
        earlier = jnp.where((lane_r < lane_c) | (lane_c >= LANES), 1.0, 0.0).astype(BF16)
        counts = dot(hot16, earlier, NN)
        rows = tiles * blocks
        row, col = iota((rows, rows), 0), iota((rows, rows), 1)
        before = (row // blocks == col // blocks) & (col < row)
        base = dot(jnp.where(before, 1.0, 0.0).astype(BF16), counts[:, LANES:].astype(BF16), NN)
        ranks = hot * (counts[:, :LANES] + base)
        rank = ranks[0:blocks]
        for t in range(1, tiles):
            rank = rank + ranks[t * blocks : (t + 1) * blocks]
        rank = rank.astype(I32)
        slot_row, slot_lane = tile * 8 + (rank >> 7), rank & 127
        cell = cell_ref[...]
        value_parts = split(values_ref[...])
        cell_parts = [(cell & mask).astype(F32) for mask in (0x7F, 0x7F << 7, 0x7 << 14)]
        sums = None
        for start in range(0, blocks, 4):
            left, right = [], []
            for b in range(start, start + 4):
                at = iota((8 * tiles, LANES), 0)
                here = at == slot_row[b : b + 1]
                there = at == slot_row[b : b + 1] + 3
                left.append(
                    jnp.concatenate(
                        [jnp.where(here, part[b : b + 1], 0.0) for part in value_parts]
                        + [jnp.where(there, part[b : b + 1], 0.0) for part in cell_parts],
                        axis=0,
                    ).astype(BF16)
                )
                right.append(jnp.where(iota((LANES, LANES), 0) == slot_lane[b : b + 1], 1.0, 0.0).astype(BF16))
            got = dot(jnp.concatenate(left, axis=1), jnp.concatenate(right, axis=1), NT)
            sums = got if sums is None else sums + got
        packed = sums[0 : 8 * tiles]
        for i in range(1, 5):
            packed = packed + sums[8 * tiles * i : 8 * tiles * (i + 1)]
        lists_out[...] = packed.reshape(tiles, 8, LANES)

    pl.semaphore_wait(barrier, mems + tiles - 2)

    def list_copy(d):
        t = other_t(d)
        return remote(lists_out.at[t], lists_in.at[me_t], list_send.at[d], list_recv.at[d], me_m, t)

    @pl.loop(1, tiles)
    def _(d):
        list_copy(d).start()

    lists_in[me_t] = lists_out[me_t]

    with jax.named_scope("prepare"):
        for copy in loads:
            copy.wait()
        to, source = iota((LAT, LAT), 0), iota((LAT, LAT), 1)
        order = jnp.where(source == (to % 8) * GROUPS + to // 8, 1.0, 0.0).astype(BF16)

        @pl.loop(0, members * FIELDS * LEVELS)
        def _(i):
            perturb[i] = dot(order, perturb_raw[i], NN).reshape(GROUPS, 8, LANES)

        for l in range(LEVELS):
            for b in range(GROUPS):
                coef_x[l, b] = coef_x_raw[l, pl.ds(b, 8, stride=GROUPS), :]
                face = coef_y_raw[l, pl.ds(b, 8, stride=GROUPS), :]
                if b == GROUPS - 1:
                    face = jnp.where(iota((8, LANES), 0) < 7, face, 0.0)
                coef_y[l, b] = face

        chunks = GROUPS // 8

        @pl.loop(0, members * FIELDS * LEVELS)
        def _(i):
            for c in range(chunks):
                edges_out[i * chunks + c] = pack_edges(lambda g: perturb[i, c * 8 + g])

        for l in range(LEVELS):
            for c in range(chunks):
                edges_out[(members * FIELDS * LEVELS + l) * chunks + c] = pack_edges(lambda g: coef_x[l, c * 8 + g])

    @pl.loop(1, tiles)
    def _(d):
        list_copy(d).wait_recv()

    edge_copies = [
        remote(edges_out, edges_in.at[1], edge_send.at[0], edge_recv.at[1], me_m, west),
        remote(edges_out, edges_in.at[0], edge_send.at[1], edge_recv.at[0], me_m, east),
    ]
    for copy in edge_copies:
        copy.start()

    def part_copy(m):
        return remote(partial.at[m], partial_in.at[me_m], part_send.at[m], part_recv.at[me_m], m, me_t)

    with jax.named_scope("deposit"):
        lists = lists_in[...]
        cells = lists.astype(I32)
        grid_row, grid_col = cells >> 7, cells & 127
        grid_row = (grid_row & ~255) | ((grid_row & 31) << 3) | ((grid_row >> 5) & 7)
        high, low = split(lists)
        per_list = CAP // LANES
        for t in range(tiles):
            for j in range(per_list):
                k = (t * per_list + j) * LANES
                here = iota((LANES, LANES), 0) == grid_col[t, 3 + j : 4 + j]
                columns[0:LANES, k : k + LANES] = jnp.where(here, high[t, j : j + 1], 0.0).astype(BF16)
                columns[LANES : 2 * LANES, k : k + LANES] = jnp.where(here, low[t, j : j + 1], 0.0).astype(BF16)

        @pl.loop(0, 4)
        def _(i):
            quarter = lax.rem(me_m // (mems // 4) + i, 4)
            at = iota((256, LANES), 0) + quarter * 256
            for t in range(0, tiles, 2):
                left = jnp.concatenate(
                    [
                        jnp.where(at == grid_row[u, 3 + j : 4 + j], 1.0, 0.0).astype(BF16)
                        for u in (t, t + 1)
                        for j in range(per_list)
                    ],
                    axis=1,
                )
                got = dot(left, columns[:, t * CAP : (t + 2) * CAP], NT)
                total[...] = got if t == 0 else total[...] + got
            whole = total[:, :LANES] + total[:, LANES:]
            for part in range(mems // 4):
                m = quarter * (mems // 4) + part
                rows = 8 * slice_vecs
                piece = whole[part * rows : (part + 1) * rows].reshape(slice_vecs, 8, LANES)
                partial[m] = piece

                @pl.when(m != me_m)
                def _():
                    part_copy(m).start()

    with jax.named_scope("halos"):
        for copy in edge_copies:
            copy.wait_recv()

        @pl.loop(0, members * FIELDS * LEVELS)
        def _(i):
            for c in range(chunks):
                merged = merge_edges(edges_in[0, i * chunks + c], edges_in[1, i * chunks + c])

                def store(g, x):
                    perturb_halo[i, c * 8 + g] = x

                unpack_edges(merged, store)

        for l in range(LEVELS):
            for c in range(chunks):
                at_edge = (members * FIELDS * LEVELS + l) * chunks + c

                def store(g, x):
                    coef_x_halo[l, c * 8 + g] = x

                unpack_edges(merge_edges(edges_in[0, at_edge], edges_in[1, at_edge]), store)

    def from_m(dst, send, recv, m):
        return remote(dst.at[m], dst.at[m], send.at[m], recv.at[m], m, me_t)

    with jax.named_scope("field_sum"):
        field = partial[me_m]

        def add(d, acc):
            m = other_m(d)
            from_m(partial_in, part_send, part_recv, m).wait_recv()
            return acc + partial_in[m]

        field = lax.fori_loop(1, mems, add, field)
        adjoint[me_m] = field

    def adj_copy(d):
        return remote(adjoint.at[me_m], adjoint.at[me_m], adj_send.at[d], adj_recv.at[me_m], other_m(d), me_t)

    def all_copy(d):
        return remote(all_edges.at[me_m], all_edges.at[me_m], all_send.at[d], all_recv.at[me_m], other_m(d), me_t)

    packs = slice_vecs // 8
    for c in range(packs):
        own_edges[c] = pack_edges(lambda g: field[c * 8 + g])
    own_copies = [
        remote(own_edges, near_edges.at[1], own_send.at[0], own_recv.at[1], me_m, west),
        remote(own_edges, near_edges.at[0], own_send.at[1], own_recv.at[0], me_m, east),
    ]
    for copy in own_copies:
        copy.start()

    @pl.loop(1, mems)
    def _(d):
        adj_copy(d).start()

    for copy in own_copies:
        copy.wait_recv()
    for c in range(packs):
        all_edges[me_m, c] = merge_edges(near_edges[0, c], near_edges[1, c])

    @pl.loop(1, mems)
    def _(d):
        all_copy(d).start()

    @pl.loop(1, mems)
    def _(d):
        m = other_m(d)
        from_m(adjoint, adj_send, adj_recv, m).wait_recv()
        from_m(all_edges, all_send, all_recv, m).wait_recv()

    with jax.named_scope("adjoint_halo"):

        @pl.loop(0, BLOCKS // 8)
        def _(i):
            def store(g, x):
                adjoint_halo[i // packs, (i % packs) * 8 + g] = x

            unpack_edges(all_edges[i // packs, i % packs], store)

    first_lane, last_lane = iota((8, LANES), 1) == 0, iota((8, LANES), 1) == LANES - 1

    def east_steps(l):
        @pl.loop(0, GROUPS)
        def _(b):
            adj, adj_h = [], []
            for f in range(FIELDS):
                vector = (f * LEVELS + l) * GROUPS + b
                adj.append(adjoint[vector // slice_vecs, vector % slice_vecs])
                adj_h.append(adjoint_halo[vector // slice_vecs, vector % slice_vecs])
            c, ch = coef_x[l, b], coef_x_halo[l, b]
            for k in range(members):
                v = vh = 0.0
                for f in range(FIELDS):
                    i = (k * FIELDS + f) * LEVELS + l
                    v = v + perturb[i, b] * adj[f]
                    vh = vh + perturb_halo[i, b] * adj_h[f]
                for _ in range(SWEEPS):
                    near, near_h = pltpu.roll(v, LANES - 1, 1), pltpu.roll(vh, LANES - 1, 1)
                    flux = c * (jnp.where(last_lane, near_h, near) - v)
                    flux_h = ch * (jnp.where(last_lane, near, near_h) - vh)
                    back, back_h = pltpu.roll(flux, 1, 1), pltpu.roll(flux_h, 1, 1)
                    v = v + flux - jnp.where(first_lane, back_h, back)
                    vh = vh + flux_h - jnp.where(first_lane, back, back_h)
                product[l * members + k, b] = v

    def north_steps(l):
        @pl.loop(0, members)
        def _(k):
            v = [product[l * members + k, b] for b in range(GROUPS)]
            for _ in range(SWEEPS):
                flux = [
                    coef_y[l, b] * ((v[b + 1] if b + 1 < GROUPS else pltpu.roll(v[0], 7, 0)) - v[b])
                    for b in range(GROUPS)
                ]
                v = [
                    v[b] + flux[b] - (flux[b - 1] if b else pltpu.roll(flux[GROUPS - 1], 1, 0))
                    for b in range(GROUPS)
                ]
            for b in range(GROUPS):
                product[l * members + k, b] = v[b]

    def increments(l):
        @pl.loop(0, GROUPS)
        def _(b):
            weights = [product[l * members + k, b] for k in range(members)]
            for f in range(FIELDS):
                acc = weights[0] * perturb[f * LEVELS + l, b]
                for k in range(1, members):
                    acc = acc + weights[k] * perturb[(k * FIELDS + f) * LEVELS + l, b]
                terms[l, pl.ds(2 * b + f, 8, stride=2 * GROUPS), :] = acc

    term_rows = 2 * LAT // mems

    def term_slice(ref, l, m):
        return ref.at[l, pl.ds(pl.multiple_of(m * term_rows, term_rows), term_rows)]

    def term_copy(l, d):
        m = other_m(d)
        return remote(
            term_slice(terms, l, m), term_slice(terms_in, l, me_m),
            term_send.at[l, d], term_recv.at[l, d], m, me_t,
        )

    for l in range(LEVELS):
        with jax.named_scope("east"):
            east_steps(l)
        with jax.named_scope("north"):
            north_steps(l)
        with jax.named_scope("increments"):
            increments(l)

        @pl.loop(1, mems)
        def _(d):
            term_copy(l, d).start()

    with jax.named_scope("increment_sum"):
        for l in range(LEVELS):
            mine = pl.ds(pl.multiple_of(me_m * term_rows, term_rows), term_rows)
            acc = terms[l, mine]

            def add(d, acc):
                term_copy(l, d).wait_recv()
                m = lax.rem(me_m + mems - d, mems)
                return acc + terms_in[l, pl.ds(pl.multiple_of(m * term_rows, term_rows), term_rows)]

            acc = lax.fori_loop(1, mems, add, acc)
            out_ref[l] = acc * (1.0 / (members * mems - 1))

    for copy in edge_copies + own_copies:
        copy.wait_send()

    @pl.loop(1, tiles)
    def _(d):
        list_copy(d).wait_send()

    @pl.loop(1, mems)
    def _(d):
        part_copy(other_m(d)).wait_send()
        adj_copy(d).wait_send()
        all_copy(d).wait_send()
        for l in range(LEVELS):
            term_copy(l, d).wait_send()


def on_device(perturb, coef_x, coef_y, obs_values, obs_tile, obs_cell):
    mems, tiles = lax.axis_size("mem"), lax.axis_size("tile")
    members = perturb.shape[0]
    channels = members * FIELDS * LEVELS
    slice_vecs = BLOCKS // mems
    edge_vecs = (channels + LEVELS) * GROUPS // 8
    term_rows = 2 * LAT // mems
    dma = pltpu.SemaphoreType.DMA

    def vectors(*shape):
        return pltpu.VMEM((*shape, 8, LANES), F32)

    out = pl.pallas_call(
        functools.partial(kernel, mems=mems, tiles=tiles, members=members),
        out_shape=jax.ShapeDtypeStruct((LEVELS, term_rows, LANES), F32),
        in_specs=[pl.BlockSpec(memory_space=pl.ANY)] * 3 + [pl.BlockSpec(memory_space=pltpu.VMEM)] * 3,
        out_specs=pl.BlockSpec(memory_space=pltpu.VMEM),
        scratch_shapes=[
            pltpu.VMEM((channels, LAT, LON), BF16),
            pltpu.VMEM((LEVELS, LAT, LON), F32),
            pltpu.VMEM((LEVELS, LAT, LON), F32),
            vectors(channels, GROUPS),
            vectors(channels, GROUPS),
            vectors(LEVELS, GROUPS),
            vectors(LEVELS, GROUPS),
            vectors(LEVELS, GROUPS),
            vectors(tiles),
            vectors(tiles),
            pltpu.VMEM((2 * LANES, tiles * CAP), BF16),
            pltpu.VMEM((256, 2 * LANES), F32),
            vectors(mems, slice_vecs),
            vectors(mems, slice_vecs),
            vectors(mems, slice_vecs),
            vectors(mems, slice_vecs),
            vectors(edge_vecs),
            vectors(2, edge_vecs),
            vectors(slice_vecs // 8),
            vectors(2, slice_vecs // 8),
            vectors(mems, slice_vecs // 8),
            vectors(LEVELS * members, GROUPS),
            pltpu.VMEM((LEVELS, 2 * LAT, LANES), F32),
            pltpu.VMEM((LEVELS, 2 * LAT, LANES), F32),
            dma((3,)),
            dma((tiles,)), dma((tiles,)),
            dma((2,)), dma((2,)),
            dma((mems,)), dma((mems,)),
            dma((mems,)), dma((mems,)),
            dma((2,)), dma((2,)),
            dma((mems,)), dma((mems,)),
            dma((LEVELS, mems)), dma((LEVELS, mems)),
        ],
        compiler_params=pltpu.CompilerParams(
            collective_id=0, has_side_effects=True, vmem_limit_bytes=56 * 2**20
        ),
    )(
        perturb.reshape(channels, LAT, LON),
        coef_x,
        coef_y,
        obs_values.reshape(-1, LANES),
        obs_tile.reshape(-1, LANES),
        obs_cell.reshape(-1, LANES),
    )
    out = out.reshape(LEVELS, LAT // mems, FIELDS, LANES)
    return jnp.transpose(out, (1, 2, 0, 3))


def solution(mesh):
    return jax.shard_map(
        on_device,
        mesh=mesh,
        in_specs=(
            P("mem", None, None, None, "tile"),
            P(None, None, "tile"),
            P(None, None, "tile"),
            P(("mem", "tile")),
            P(("mem", "tile"), None),
            P(("mem", "tile")),
        ),
        out_specs=P("mem", None, None, "tile"),
        check_vma=False,
    )
```

time: 437 us -> 112 us (0.26)
  waiting for transfers between devices: 264 us -> 0 us
  Pallas kernels: 0 us -> 111 us
  other arithmetic: 72.8 us -> 0 us
  local copies, waits for them, and re-layouts: 48.6 us -> 1.4 us
  blocking collectives: 20.4 us -> 0 us
  starting transfers between devices: 16.5 us -> 0 us
  between operations: 14.4 us -> 0.01 us
    unnamed x3 -> x0, waiting for transfers between devices: 122 us -> none
    psum x1 -> x0, waiting for transfers between devices: 119 us -> none  [on_device(): adjoint_field = lax.psum(deposit(incoming, total_cells), 'mem')]
    pallas_call x0 -> x1, Pallas kernels: none -> 111 us  [on_device(): pl.pallas_call(functools.partial(kernel, mems=mems, tiles=tiles, members=...]
    scatter-add x1 -> x0, other arithmetic: 41.6 us -> none  [deposit(): return jnp.zeros((total_cells,), jnp.float32).at[cells].add(lists[0])]
    ppermute x12 -> x0, waiting for transfers between devices: 22.7 us -> none  [the longest x6 20.2 us: extended_2(): lax.ppermute(lax.slice_in_dim(block, block.shape[dim] - width, None, axis...]
    slice x18 -> x0, local copies, waits for them, and re-layouts: 22.2 us -> none  [the longest x11 11.4 us: extended_2(): lax.slice_in_dim(block, block.shape[dim] - width, None, axis=dim)]
    all_to_all x1 -> x0, blocking collectives: 20.4 us -> none  [on_device(): lax.all_to_all(outgoing, 'tile', split_axis=1, concat_axis=1, tiled=True)]
    ppermute x12 -> x0, starting transfers between devices: 16.5 us -> none  [the longest x6 8.7 us: extended_2(): lax.ppermute(lax.slice_in_dim(block, 0, width, axis=dim), axis, backward)]
  transfers between devices with their start and end apart: 14 -> 0, of which waited for: 12 -> 0; matrix products, arithmetic and copies ran while one was open for 2% -> 0% of each run, Pallas kernels for 0% -> 0%
where the time goes in v1:
time: 112 us
  Pallas kernels  111 us (99%)
  local copies, waits for them, and re-layouts  1.4 us (1%)
    pallas_call x1, Pallas kernels, on_device(): pl.pallas_call(functools.partial(kernel, mems=mems, tiles=tiles, members=...  111 us

profile of v1, /device:TPU:1, one launch (start us, length us, event | category | flops | bytes accessed | tf_op | source)
XLA Modules:
  0.0 112.2 jit_solution(12080184225819232240)
XLA Ops:
  0.0 110.7 %shard_map.64 = f32[2,32,128]{2,1,0:T(8,128)} custom-call(bf16[20,256,128]{2,1,0:T(8,128)(2,1)} %bitcast.8, f32[2,256,128]{2,1,0:T(8,128)} %coef_x_hbm.1, f32[2,256,128]{2,1,0:T(8,128)} %coef_y_hbm.1, f32[16,128]{1,0:T(8,128)} %bitcast.10, s32[16,128]{1,0:T(8,128)} %bitcast.11, s32[16,128]{1,0:T(8,128)} %bitcast.12), custom_call_target="tpu_custom_call" | custom-call | tf_op jit(solution)/shard_map/pallas_call | solution.py:439
  110.8 1.4 %copy.9 = f32[2,16,2,128]{3,0,2,1:T(2,128)} copy(f32[2,16,2,128]{3,2,1,0:T(2,128)} %bitcast.9) | data formatting | bytes 65536 | tf_op jit(solution)/shard_map/reshape | solution.py:489

commit v2 on v0

v2 whole, which is shorter than its diff:
```python
import functools

import jax
import jax.numpy as jnp
from jax import lax
from jax.experimental import pallas as pl
from jax.experimental.pallas import tpu as pltpu
from jax.sharding import PartitionSpec as P

FIELDS = 2
LEVELS = 2
SWEEPS = 6
LAT = 256
LON = 128
CAP = 384
LANES = 128
GROUPS = LAT // 8
HALO = 8
WIDE = LON + 2 * HALO
STEPS = WIDE // 8
HALVES = LAT // LANES
CHIPS = 8
PART = LON // 4
F32 = jnp.float32
BF16 = jnp.bfloat16
I32 = jnp.int32
NT = (((1,), (1,)), ((), ()))
NN = (((1,), (0,)), ((), ()))


def iota(shape, dim):
    return lax.broadcasted_iota(I32, shape, dim)


def dot(a, b, dims):
    return lax.dot_general(a, b, dims, preferred_element_type=F32)


def split(x):
    high = x.astype(BF16).astype(F32)
    return high, x - high


def kernel(
    perturb_hbm, coef_x_hbm, coef_y_hbm, values_ref, tile_ref, cell_ref, out_ref,
    perturb_raw, coef_x_raw, coef_y_raw, perturb, perturb_t, perturb_g, coef_t, coef_g, coef_y,
    lists_out, lists_in, columns, total, partial, sibling_in, partial_in, adjoint_t, adjoint_g,
    diffused, product, terms, terms_sibling, terms_in,
    load_sem, list_send, list_recv, edge_send, edge_recv, half_send, half_recv, part_send, part_recv,
    adj_send, adj_recv, pass_send, pass_recv, halo_send, halo_recv, halo_pass_send, halo_pass_recv,
    near_send, near_recv, term_send, term_recv,
    *, tiles, members,
):
    me_m, me_t = lax.axis_index("mem"), lax.axis_index("tile")
    chip, core = me_m // 2, lax.rem(me_m, 2)
    sibling = 2 * chip + 1 - core
    west, east = lax.rem(me_t + tiles - 1, tiles), lax.rem(me_t + 1, tiles)
    blocks = values_ref.shape[0]
    channels = members * FIELDS * LEVELS

    def remote(src, dst, send, recv, m, t):
        return pltpu.make_async_remote_copy(
            src_ref=src, dst_ref=dst, send_sem=send, recv_sem=recv,
            device_id={"mem": m, "tile": t}, device_id_type=pl.DeviceIdType.MESH,
        )

    def signal(m, t):
        pl.semaphore_signal(
            barrier, 1, device_id={"mem": m, "tile": t}, device_id_type=pl.DeviceIdType.MESH
        )

    def other_chip(d):
        return lax.rem(chip + d, CHIPS)

    def other_t(d):
        return lax.rem(me_t + d, tiles)

    loads = [
        pltpu.make_async_copy(src, dst, load_sem.at[i])
        for i, (src, dst) in enumerate(
            ((perturb_hbm, perturb_raw), (coef_x_hbm, coef_x_raw), (coef_y_hbm, coef_y_raw))
        )
    ]
    for copy in loads:
        copy.start()

    barrier = pltpu.get_barrier_semaphore()
    signal(sibling, me_t)

    @pl.loop(1, CHIPS)
    def _(d):
        m = 2 * other_chip(d) + core
        signal(m, me_t)
        signal(m, west)
        signal(m, east)

    @pl.loop(1, tiles)
    def _(d):
        signal(me_m, other_t(d))

    with jax.named_scope("bucket"):
        tile = tile_ref[...]
        hot = jnp.concatenate([jnp.where(tile == t, 1.0, 0.0) for t in range(tiles)], axis=0)
        hot16 = hot.astype(BF16)
        lane_r, lane_c = iota((LANES, 2 * LANES), 0), iota((LANES, 2 * LANES), 1)
        earlier = jnp.where((lane_r < lane_c) | (lane_c >= LANES), 1.0, 0.0).astype(BF16)
        counts = dot(hot16, earlier, NN)
        rows = tiles * blocks
        row, col = iota((rows, rows), 0), iota((rows, rows), 1)
        before = (row // blocks == col // blocks) & (col < row)
        base = dot(jnp.where(before, 1.0, 0.0).astype(BF16), counts[:, LANES:].astype(BF16), NN)
        ranks = hot * (counts[:, :LANES] + base)
        rank = ranks[0:blocks]
        for t in range(1, tiles):
            rank = rank + ranks[t * blocks : (t + 1) * blocks]
        rank = rank.astype(I32)
        slot_row, slot_lane = tile * 8 + (rank >> 7), rank & 127
        cell = cell_ref[...]
        value_parts = split(values_ref[...])
        cell_parts = [(cell & mask).astype(F32) for mask in (0x7F, 0x7F << 7, 0x7 << 14)]
        sums = None
        for start in range(0, blocks, 4):
            left, right = [], []
            for b in range(start, start + 4):
                at = iota((8 * tiles, LANES), 0)
                here = at == slot_row[b : b + 1]
                there = at == slot_row[b : b + 1] + 3
                left.append(
                    jnp.concatenate(
                        [jnp.where(here, part[b : b + 1], 0.0) for part in value_parts]
                        + [jnp.where(there, part[b : b + 1], 0.0) for part in cell_parts],
                        axis=0,
                    ).astype(BF16)
                )
                right.append(jnp.where(iota((LANES, LANES), 0) == slot_lane[b : b + 1], 1.0, 0.0).astype(BF16))
            got = dot(jnp.concatenate(left, axis=1), jnp.concatenate(right, axis=1), NT)
            sums = got if sums is None else sums + got
        packed = sums[0 : 8 * tiles]
        for i in range(1, 5):
            packed = packed + sums[8 * tiles * i : 8 * tiles * (i + 1)]
        lists_out[...] = packed.reshape(tiles, 8, LANES)

    for copy in loads:
        copy.wait()
    with jax.named_scope("prepare"):
        to, source = iota((LAT, LAT), 0), iota((LAT, LAT), 1)
        order = jnp.where(source == (to % 8) * GROUPS + to // 8, 1.0, 0.0).astype(BF16)
        same = jnp.where(iota((LON, LON), 0) == iota((LON, LON), 1), 1.0, 0.0).astype(BF16)

        @pl.loop(0, channels)
        def _(i):
            rows = dot(order, perturb_raw[i], NN)
            perturb[i] = rows.reshape(GROUPS, 8, LANES)
            turned = dot(same, rows.astype(BF16), NT)
            for h in range(HALVES):
                perturb_t[i, h, HALO : HALO + LON] = turned[:, h * LANES : (h + 1) * LANES]

        for l in range(LEVELS):
            faces = []
            for b in range(GROUPS):
                faces.append(coef_x_raw[l, pl.ds(b, 8, stride=GROUPS), :])
                face = coef_y_raw[l, pl.ds(b, 8, stride=GROUPS), :]
                if b == GROUPS - 1:
                    face = jnp.where(iota((8, LANES), 0) < 7, face, 0.0)
                coef_y[l, b] = face
            faces = jnp.concatenate(faces, axis=0)
            for h in range(HALVES):
                coef_t[l, h, HALO : HALO + LON] = faces[h * LANES : (h + 1) * LANES].T

    pl.semaphore_wait(barrier, 1 + 3 * (CHIPS - 1) + tiles - 1)

    def list_copy(d):
        t = other_t(d)
        return remote(lists_out.at[t], lists_in.at[me_t], list_send.at[d], list_recv.at[d], me_m, t)

    @pl.loop(1, tiles)
    def _(d):
        list_copy(d).start()

    lists_in[me_t] = lists_out[me_t]

    def edge(ref, start):
        return ref.at[:, :, pl.ds(start, HALO)]

    edge_copies = []
    for i, ref in enumerate((perturb_t, coef_t)):
        edge_copies.append(
            remote(edge(ref, LON), edge(ref, 0), edge_send.at[i, 0], edge_recv.at[i, 0], me_m, east)
        )
        edge_copies.append(
            remote(edge(ref, HALO), edge(ref, HALO + LON), edge_send.at[i, 1], edge_recv.at[i, 1], me_m, west)
        )
    for copy in edge_copies:
        copy.start()

    @pl.loop(1, tiles)
    def _(d):
        list_copy(d).wait_recv()

    half_copy = remote(partial.at[1 - core], sibling_in, half_send.at[0], half_recv.at[0], sibling, me_t)

    with jax.named_scope("deposit"):
        lists = lists_in[...]
        cells = lists.astype(I32)
        grid_row = (cells >> 15) * LON + (cells & (LON - 1))
        grid_lane = (cells >> 7) & (LAT - 1)
        grid_lane = (grid_lane % GROUPS) * 8 + grid_lane // GROUPS
        high, low = split(lists)
        per_list = CAP // LANES
        for t in range(tiles):
            for j in range(per_list):
                k = (t * per_list + j) * LANES
                here = iota((LAT, LANES), 0) == grid_lane[t, 3 + j : 4 + j]
                columns[0:LAT, k : k + LANES] = jnp.where(here, high[t, j : j + 1], 0.0).astype(BF16)
                columns[LAT : 2 * LAT, k : k + LANES] = jnp.where(here, low[t, j : j + 1], 0.0).astype(BF16)
        span = 4
        for f in (1 - core, core):
            at = iota((2 * LON, LANES), 0) + f * (2 * LON)
            for t in range(0, tiles, span):
                left = jnp.concatenate(
                    [
                        jnp.where(at == grid_row[u, 3 + j : 4 + j], 1.0, 0.0).astype(BF16)
                        for u in range(t, t + span)
                        for j in range(per_list)
                    ],
                    axis=1,
                )
                got = dot(left, columns[:, t * CAP : (t + span) * CAP], NT)
                if t == 0:
                    total[...] = got
                elif t + span < tiles:
                    total[...] += got
            for h in range(HALVES):
                lanes = slice(h * LANES, (h + 1) * LANES)
                lows = slice(LAT + h * LANES, LAT + (h + 1) * LANES)
                partial[f, h] = (total[:, lanes] + got[:, lanes]) + (total[:, lows] + got[:, lows])
            if f is not core:
                half_copy.start()

    def rows(c):
        return pl.ds(pl.multiple_of(c * PART, PART), PART)

    def part_copy(d):
        c = other_chip(d)
        return remote(
            partial.at[core, :, rows(c)], partial_in.at[chip], part_send.at[d], part_recv.at[d], 2 * c + core, me_t
        )

    half_copy.wait_recv()
    with jax.named_scope("sibling_sum"):
        for h in range(HALVES):
            partial[core, h] += sibling_in[h]

    @pl.loop(1, CHIPS)
    def _(d):
        part_copy(d).start()

    for copy in edge_copies:
        copy.wait_recv()

    def gather(source, target, i):
        for h in range(HALVES):
            for b in range(STEPS):
                target[i, h, b] = source[i, h, pl.ds(b, 8, stride=STEPS), :]

    with jax.named_scope("gather"):

        @pl.loop(0, channels)
        def _(i):
            gather(perturb_t, perturb_g, i)

        for l in range(LEVELS):
            gather(coef_t, coef_g, l)

    def block(f, c):
        start = pl.multiple_of(HALO + lax.rem(c, 4) * PART, 8)
        return adjoint_t.at[f * LEVELS + c // 4, :, pl.ds(start, PART)]

    field = partial[core, :, rows(chip)]

    def add_part(d, acc):
        part_copy(d).wait_recv()
        return acc + partial_in[other_chip(CHIPS - d)]

    block(core, chip)[...] = lax.fori_loop(1, CHIPS, add_part, field)

    def adj_copy(d):
        mine = block(core, chip)
        return remote(mine, mine, adj_send.at[d], adj_recv.at[chip], 2 * other_chip(d) + core, me_t)

    def adj_from(c):
        there = block(core, c)
        return remote(there, there, adj_send.at[0], adj_recv.at[c], 2 * other_chip(1) + core, me_t)

    def pass_copy(c, f):
        there = block(f, c)
        return remote(there, there, pass_send.at[c], pass_recv.at[c], sibling, me_t)

    def halo_at(f, l, start):
        return adjoint_t.at[f * LEVELS + l, :, pl.ds(start, HALO)]

    def halo_copy(c, side):
        l = chip // 4
        source = halo_at(core, l, HALO if side else LON)
        target = halo_at(core, l, HALO + LON if side else 0)
        return remote(
            source, target, halo_send.at[c], halo_recv.at[l, side], 2 * c + core, west if side else east
        )

    def halo_from(l, side):
        target = halo_at(core, l, HALO + LON if side else 0)
        return remote(target, target, halo_send.at[0], halo_recv.at[l, side], me_m, east)

    def halo_pass(f, l, side):
        target = halo_at(f, l, HALO + LON if side else 0)
        return remote(target, target, halo_pass_send.at[l, side], halo_pass_recv.at[l, side], sibling, me_t)

    @pl.loop(1, CHIPS)
    def _(d):
        adj_copy(d).start()

    for side in (0, 1):

        @pl.when(lax.rem(chip, 4) == (0 if side else 3))
        def _():
            @pl.loop(0, CHIPS)
            def _(c):
                halo_copy(c, side).start()

    pass_copy(chip, core).start()

    @pl.loop(1, CHIPS)
    def _(d):
        c = other_chip(d)
        adj_from(c).wait_recv()
        pass_copy(c, core).start()

    for l in range(LEVELS):
        for side in (0, 1):
            halo_from(l, side).wait_recv()
            halo_pass(core, l, side).start()

    def east_steps(l):
        for h in range(HALVES):
            for f in range(FIELDS):
                for b in range(STEPS):
                    adjoint_g[f, h, b] = adjoint_t[f * LEVELS + l, h, pl.ds(b, 8, stride=STEPS), :]

        for h in range(HALVES):

            @pl.loop(0, members)
            def _(k):
                i = k * (FIELDS * LEVELS) + l
                v = [
                    perturb_g[i, h, b] * adjoint_g[0, h, b] + perturb_g[i + LEVELS, h, b] * adjoint_g[1, h, b]
                    for b in range(STEPS)
                ]
                for _ in range(SWEEPS):
                    following = v[1:] + [pltpu.roll(v[0], 7, 0)]
                    flux = [coef_g[l, h, b] * (following[b] - v[b]) for b in range(STEPS)]
                    before = [pltpu.roll(flux[-1], 1, 0)] + flux[:-1]
                    v = [v[b] + flux[b] - before[b] for b in range(STEPS)]
                for b in range(STEPS):
                    diffused[k, h, pl.ds(b, 8, stride=STEPS), :] = v[b]

    def turn(l):
        @pl.loop(0, members)
        def _(k):
            for h in range(HALVES):
                turned = diffused[k, h, HALO : HALO + LON].T
                half = GROUPS // HALVES
                product[l * members + k, h * half : (h + 1) * half] = turned.reshape(half, 8, LANES)

    def north_steps(l):
        @pl.loop(0, members)
        def _(k):
            v = [product[l * members + k, b] for b in range(GROUPS)]
            for _ in range(SWEEPS):
                following = v[1:] + [pltpu.roll(v[0], 7, 0)]
                flux = [coef_y[l, b] * (following[b] - v[b]) for b in range(GROUPS)]
                before = [pltpu.roll(flux[-1], 1, 0)] + flux[:-1]
                v = [v[b] + flux[b] - before[b] for b in range(GROUPS)]
            for b in range(GROUPS):
                product[l * members + k, b] = v[b]

    share = LAT // (2 * CHIPS)

    def increments(l, half):
        @pl.loop(0, share)
        def _(b):
            at = half * share + b
            weights = [product[l * members + k, at] for k in range(members)]
            for f in range(FIELDS):
                acc = weights[0] * perturb[f * LEVELS + l, at]
                for k in range(1, members):
                    acc = acc + weights[k] * perturb[(k * FIELDS + f) * LEVELS + l, at]
                terms[l, half, pl.ds(2 * b + f, 8, stride=2 * share), :] = acc

    def out_rows(c):
        return pl.ds(pl.multiple_of(c * 2 * share, 2 * share), 2 * share)

    def near_copy(l):
        return remote(terms.at[l, 1 - core], terms_sibling.at[l], near_send.at[l], near_recv.at[l], sibling, me_t)

    def term_copy(l, d):
        c = other_chip(d)
        return remote(
            terms.at[l, core, out_rows(c)], terms_in.at[l, chip],
            term_send.at[l, d], term_recv.at[l, d], 2 * c + core, me_t,
        )

    def send_terms(l):
        near_copy(l).wait_recv()
        terms[l, core] += terms_sibling[l]

        @pl.loop(1, CHIPS)
        def _(d):
            term_copy(l, d).start()

    for l in range(LEVELS):
        for c in range(4 * l, 4 * l + 4):
            pass_copy(c, 1 - core).wait_recv()
        for side in (0, 1):
            halo_pass(1 - core, l, side).wait_recv()
        with jax.named_scope("east"):
            east_steps(l)
        with jax.named_scope("turn"):
            turn(l)
        if l:
            send_terms(l - 1)
        with jax.named_scope("north"):
            north_steps(l)
        with jax.named_scope("increments"):
            increments(l, 1 - core)
        near_copy(l).start()
        with jax.named_scope("increments"):
            increments(l, core)
    send_terms(LEVELS - 1)

    for l in range(LEVELS):

        def add_term(d, acc):
            term_copy(l, d).wait_recv()
            return acc + terms_in[l, other_chip(CHIPS - d)]

        acc = lax.fori_loop(1, CHIPS, add_term, terms[l, core, out_rows(chip)])
        out_ref[l] = acc * (1.0 / (2 * CHIPS * members - 1))

    for copy in edge_copies + [half_copy]:
        copy.wait_send()

    @pl.loop(1, tiles)
    def _(d):
        list_copy(d).wait_send()

    @pl.loop(1, CHIPS)
    def _(d):
        part_copy(d).wait_send()
        adj_copy(d).wait_send()
        for l in range(LEVELS):
            term_copy(l, d).wait_send()

    @pl.loop(0, CHIPS)
    def _(c):
        pass_copy(c, core).wait_send()

    for side in (0, 1):

        @pl.when(lax.rem(chip, 4) == (0 if side else 3))
        def _():
            @pl.loop(0, CHIPS)
            def _(c):
                halo_copy(c, side).wait_send()

    for l in range(LEVELS):
        near_copy(l).wait_send()
        for side in (0, 1):
            halo_pass(core, l, side).wait_send()


def on_device(perturb, coef_x, coef_y, obs_values, obs_tile, obs_cell):
    tiles = lax.axis_size("tile")
    members = perturb.shape[0]
    channels = members * FIELDS * LEVELS
    share = LAT // (2 * CHIPS)
    dma = pltpu.SemaphoreType.DMA

    def rows(*shape):
        return pltpu.VMEM((*shape, LANES), F32)

    out = pl.pallas_call(
        functools.partial(kernel, tiles=tiles, members=members),
        out_shape=jax.ShapeDtypeStruct((LEVELS, 2 * share, LANES), F32),
        in_specs=[pl.BlockSpec(memory_space=pl.ANY)] * 3 + [pl.BlockSpec(memory_space=pltpu.VMEM)] * 3,
        out_specs=pl.BlockSpec(memory_space=pltpu.VMEM),
        scratch_shapes=[
            pltpu.VMEM((channels, LAT, LON), BF16),
            rows(LEVELS, LAT),
            rows(LEVELS, LAT),
            rows(channels, GROUPS, 8),
            rows(channels, HALVES, WIDE),
            rows(channels, HALVES, STEPS, 8),
            rows(LEVELS, HALVES, WIDE),
            rows(LEVELS, HALVES, STEPS, 8),
            rows(LEVELS, GROUPS, 8),
            rows(tiles, 8),
            rows(tiles, 8),
            pltpu.VMEM((2 * LAT, tiles * CAP), BF16),
            pltpu.VMEM((LEVELS * LON, 2 * LAT), F32),
            rows(FIELDS, HALVES, LEVELS * LON),
            rows(HALVES, LEVELS * LON),
            rows(CHIPS, HALVES, PART),
            rows(FIELDS * LEVELS, HALVES, WIDE),
            rows(FIELDS, HALVES, STEPS, 8),
            rows(members, HALVES, WIDE),
            rows(LEVELS * members, GROUPS, 8),
            rows(LEVELS, 2, LAT),
            rows(LEVELS, LAT),
            rows(LEVELS, CHIPS, 2 * share),
            dma((3,)),
            dma((tiles,)), dma((tiles,)),
            dma((2, 2)), dma((2, 2)),
            dma((1,)), dma((1,)),
            dma((CHIPS,)), dma((CHIPS,)),
            dma((CHIPS,)), dma((CHIPS,)),
            dma((CHIPS,)), dma((CHIPS,)),
            dma((CHIPS,)), dma((LEVELS, 2)),
            dma((LEVELS, 2)), dma((LEVELS, 2)),
            dma((LEVELS,)), dma((LEVELS,)),
            dma((LEVELS, CHIPS)), dma((LEVELS, CHIPS)),
        ],
        compiler_params=pltpu.CompilerParams(
            collective_id=0, has_side_effects=True, vmem_limit_bytes=56 * 2**20
        ),
    )(
        perturb.reshape(channels, LAT, LON),
        coef_x,
        coef_y,
        obs_values.reshape(-1, LANES),
        obs_tile.reshape(-1, LANES),
        obs_cell.reshape(-1, LANES),
    )
    out = out.reshape(LEVELS, share, FIELDS, LANES)
    return jnp.transpose(out, (1, 2, 0, 3))


def solution(mesh):
    return jax.shard_map(
        on_device,
        mesh=mesh,
        in_specs=(
            P("mem", None, None, None, "tile"),
            P(None, None, "tile"),
            P(None, None, "tile"),
            P(("mem", "tile")),
            P(("mem", "tile"), None),
            P(("mem", "tile")),
        ),
        out_specs=P("mem", None, None, "tile"),
        check_vma=False,
    )
```

time: 437 us -> 54.7 us (0.13)
  waiting for transfers between devices: 264 us -> 0 us
  other arithmetic: 72.8 us -> 0 us
  Pallas kernels: 0 us -> 53.2 us
  local copies, waits for them, and re-layouts: 48.6 us -> 1.4 us
  blocking collectives: 20.4 us -> 0 us
  starting transfers between devices: 16.5 us -> 0 us
  between operations: 14.4 us -> 0.01 us
    unnamed x3 -> x0, waiting for transfers between devices: 122 us -> none
    psum x1 -> x0, waiting for transfers between devices: 119 us -> none  [on_device(): adjoint_field = lax.psum(deposit(incoming, total_cells), 'mem')]
    pallas_call x0 -> x1, Pallas kernels: none -> 53.2 us  [on_device(): pl.pallas_call(functools.partial(kernel, tiles=tiles, members=members), o...]
    scatter-add x1 -> x0, other arithmetic: 41.6 us -> none  [deposit(): return jnp.zeros((total_cells,), jnp.float32).at[cells].add(lists[0])]
    ppermute x12 -> x0, waiting for transfers between devices: 22.7 us -> none  [the longest x6 20.2 us: extended_2(): lax.ppermute(lax.slice_in_dim(block, block.shape[dim] - width, None, axis...]
    slice x18 -> x0, local copies, waits for them, and re-layouts: 22.2 us -> none  [the longest x11 11.4 us: extended_2(): lax.slice_in_dim(block, block.shape[dim] - width, None, axis=dim)]
    all_to_all x1 -> x0, blocking collectives: 20.4 us -> none  [on_device(): lax.all_to_all(outgoing, 'tile', split_axis=1, concat_axis=1, tiled=True)]
    ppermute x12 -> x0, starting transfers between devices: 16.5 us -> none  [the longest x6 8.7 us: extended_2(): lax.ppermute(lax.slice_in_dim(block, 0, width, axis=dim), axis, backward)]
  transfers between devices with their start and end apart: 14 -> 0, of which waited for: 12 -> 0; matrix products, arithmetic and copies ran while one was open for 2% -> 0% of each run, Pallas kernels for 0% -> 0%
where the time goes in v2:
time: 54.7 us; the launch traced here: 54.6 us
  Pallas kernels  53.2 us (97%)
  local copies, waits for them, and re-layouts  1.4 us (3%)
    pallas_call x1, Pallas kernels, on_device(): pl.pallas_call(functools.partial(kernel, tiles=tiles, members=members), o...  53.2 us
    reshape x1, local copies, waits for them, and re-layouts, on_device(): out = out.reshape(LEVELS, share, FIELDS, LANES)  1.4 us

profile of v2, /device:TPU:1, one launch (start us, length us, event | category | flops | bytes accessed | tf_op | source)
XLA Modules:
  0.0 54.6 jit_solution(15318949007325386444)
XLA Ops:
  0.0 53.2 %shard_map.64 = f32[2,32,128]{2,1,0:T(8,128)} custom-call(bf16[20,256,128]{2,1,0:T(8,128)(2,1)} %bitcast.8, f32[2,256,128]{2,1,0:T(8,128)} %coef_x_hbm.1, f32[2,256,128]{2,1,0:T(8,128)} %coef_y_hbm.1, f32[16,128]{1,0:T(8,128)} %bitcast.10, s32[16,128]{1,0:T(8,128)} %bitcast.11, s32[16,128]{1,0:T(8,128)} %bitcast.12), custom_call_target="tpu_custom_call" | custom-call | tf_op jit(solution)/shard_map/pallas_call | solution.py:491
  53.2 1.4 %copy.9 = f32[2,16,2,128]{3,0,2,1:T(2,128)} copy(f32[2,16,2,128]{3,2,1,0:T(2,128)} %bitcast.9) | data formatting | bytes 65536 | tf_op jit(solution)/shard_map/reshape | solution.py:543

commit v3 on v0

v3 whole, which is shorter than its diff:
```python
import functools

import jax
import jax.numpy as jnp
from jax import lax
from jax.experimental import pallas as pl
from jax.experimental.pallas import tpu as pltpu
from jax.sharding import PartitionSpec as P

FIELDS = 2
LEVELS = 2
SWEEPS = 6
LAT = 256
LON = 128
CAP = 384
LANES = 128
GROUPS = LAT // 8
HALO = 8
WIDE = LON + 2 * HALO
STEPS = WIDE // 8
HALVES = LAT // LANES
CHIPS = 8
DEPTH = 8
OFFSETS = ((0, 0), (0, 1), (0, 7), (0, 2), (0, 6), (1, 0), (0, 3), (0, 5), (1, 1), (1, 7), (0, 4), (1, 2), (1, 6), (1, 3), (1, 5), (1, 4))
PART = LON // 4
F32 = jnp.float32
BF16 = jnp.bfloat16
I32 = jnp.int32
NT = (((1,), (1,)), ((), ()))
NN = (((1,), (0,)), ((), ()))


def iota(shape, dim):
    return lax.broadcasted_iota(I32, shape, dim)


def dot(a, b, dims):
    return lax.dot_general(a, b, dims, preferred_element_type=F32)


def split(x):
    high = x.astype(BF16).astype(F32)
    return high, x - high


def kernel(
    perturb_hbm, coef_x_hbm, coef_y_hbm, values_ref, tile_ref, cell_ref, out_ref,
    perturb_raw, coef_x_raw, coef_y_raw, perturb, perturb_out, perturb_t, perturb_g, coef_t, coef_g, coef_y,
    lists_out, lists_in, total, partial, partial_in, adjoint_t, adjoint_g, diffused, product, terms, terms_in,
    load_sem, list_send, list_recv, share_send, share_recv, edge_send, edge_recv, part_send, part_recv,
    adj_send, adj_recv, halo_send, halo_recv, term_send, term_recv,
    *, tiles, members,
):
    me_m, me_t = lax.axis_index("mem"), lax.axis_index("tile")
    chip, core = me_m // 2, lax.rem(me_m, 2)
    sibling = 2 * chip + 1 - core
    west, east = lax.rem(me_t + tiles - 1, tiles), lax.rem(me_t + 1, tiles)
    blocks = values_ref.shape[0]
    mems = 2 * CHIPS
    own = members * FIELDS

    def remote(src, dst, send, recv, m, t):
        return pltpu.make_async_remote_copy(
            src_ref=src, dst_ref=dst, send_sem=send, recv_sem=recv,
            device_id={"mem": m, "tile": t}, device_id_type=pl.DeviceIdType.MESH,
        )

    def signal(m, t):
        pl.semaphore_signal(
            barrier, 1, device_id={"mem": m, "tile": t}, device_id_type=pl.DeviceIdType.MESH
        )

    def other_chip(d):
        return lax.rem(chip + d, CHIPS)

    def other_m(d):
        return lax.rem(me_m + d, mems)

    loads = [
        pltpu.make_async_copy(src, dst, load_sem.at[i])
        for i, (src, dst) in enumerate(
            (
                (perturb_hbm.at[:, 1 - core], perturb_raw.at[:, 1 - core]),
                (perturb_hbm.at[:, core], perturb_raw.at[:, core]),
                (coef_x_hbm.at[core], coef_x_raw),
                (coef_y_hbm.at[core], coef_y_raw),
            )
        )
    ]
    for copy in loads:
        copy.start()

    barrier = pltpu.get_barrier_semaphore()
    signal(sibling, me_t)

    @pl.loop(1, tiles)
    def _(d):
        t = lax.rem(me_t + d, tiles)
        signal(me_m, t)
        signal(sibling, t)

    @pl.loop(1, CHIPS)
    def _(d):
        m = 2 * other_chip(d) + core
        signal(m, me_t)
        signal(2 * other_chip(d) + 1 - core, me_t)
        signal(m, west)
        signal(m, east)

    with jax.named_scope("bucket"):
        tile = tile_ref[...]
        hot = jnp.concatenate([jnp.where(tile == t, 1.0, 0.0) for t in range(tiles)], axis=0)
        hot16 = hot.astype(BF16)
        lane_r, lane_c = iota((LANES, 2 * LANES), 0), iota((LANES, 2 * LANES), 1)
        earlier = jnp.where((lane_r < lane_c) | (lane_c >= LANES), 1.0, 0.0).astype(BF16)
        counts = dot(hot16, earlier, NN)
        rows = tiles * blocks
        row, col = iota((rows, rows), 0), iota((rows, rows), 1)
        before = (row // blocks == col // blocks) & (col < row)
        base = dot(jnp.where(before, 1.0, 0.0).astype(BF16), counts[:, LANES:].astype(BF16), NN)
        ranks = hot * (counts[:, :LANES] + base)
        rank = ranks[0:blocks]
        for t in range(1, tiles):
            rank = rank + ranks[t * blocks : (t + 1) * blocks]
        rank = rank.astype(I32)
        slot_row, slot_lane = tile * 8 + (rank >> 7), rank & 127
        cell = cell_ref[...]
        value_parts = split(values_ref[...])
        cell_parts = [(cell & mask).astype(F32) for mask in (0x7F, 0x7F << 7, 0x7 << 14)]
        sums = None
        for start in range(0, blocks, 4):
            left, right = [], []
            for b in range(start, start + 4):
                at = iota((8 * tiles, LANES), 0)
                here = at == slot_row[b : b + 1]
                there = at == slot_row[b : b + 1] + 3
                left.append(
                    jnp.concatenate(
                        [jnp.where(here, part[b : b + 1], 0.0) for part in value_parts]
                        + [jnp.where(there, part[b : b + 1], 0.0) for part in cell_parts],
                        axis=0,
                    ).astype(BF16)
                )
                right.append(jnp.where(iota((LANES, LANES), 0) == slot_lane[b : b + 1], 1.0, 0.0).astype(BF16))
            got = dot(jnp.concatenate(left, axis=1), jnp.concatenate(right, axis=1), NT)
            sums = got if sums is None else sums + got
        packed = sums[0 : 8 * tiles]
        for i in range(1, 5):
            packed = packed + sums[8 * tiles * i : 8 * tiles * (i + 1)]
        lists_out[...] = packed.reshape(tiles, 8, LANES)
    pl.semaphore_wait(barrier, 1 + 2 * (tiles - 1) + 4 * (CHIPS - 1))

    def list_copy(n, to):
        y, z = OFFSETS[n]
        t = lax.rem(me_t // DEPTH + y, 2) * DEPTH + lax.rem(me_t + DEPTH - z, DEPTH)
        return remote(
            lists_out.at[t], lists_in.at[2 * n + core], list_send.at[n, to], list_recv.at[2 * n + core],
            2 * chip + to, t,
        )

    to_sibling = remote(
        lists_out.at[me_t], lists_in.at[core], list_send.at[0, 0], list_recv.at[core], sibling, me_t
    )
    for n in range(tiles - 1, 0, -1):
        for to in range(2):
            list_copy(n, to).start()
    to_sibling.start()
    lists_in[core] = lists_out[me_t]

    to, source = iota((LAT, LAT), 0), iota((LAT, LAT), 1)
    order = jnp.where(source == (to % 8) * GROUPS + to // 8, 1.0, 0.0).astype(BF16)
    same = jnp.where(iota((LON, LON), 0) == iota((LON, LON), 1), 1.0, 0.0).astype(BF16)

    def ordered(l, f):
        side = jnp.concatenate([perturb_raw[k * FIELDS + f, l] for k in range(members)], axis=1)
        got = dot(order, side, NN)
        return [got[:, k * LON : (k + 1) * LON] for k in range(members)]

    def turn_in(i, x):
        turned = dot(same, x.astype(BF16), NT)
        for h in range(HALVES):
            perturb_t[i, h, HALO : HALO + LON] = turned[:, h * LANES : (h + 1) * LANES]

    share_copy = remote(perturb_out, perturb.at[pl.ds(own, own)], share_send.at[0], share_recv.at[0], sibling, me_t)
    loads[0].wait()
    with jax.named_scope("share"):
        for f in range(FIELDS):
            for k, x in enumerate(ordered(1 - core, f)):
                perturb_out[k * FIELDS + f] = x.reshape(GROUPS, 8, LANES)
    share_copy.start()
    for copy in loads[1:]:
        copy.wait()
    with jax.named_scope("prepare"):
        for f in range(FIELDS):
            for k, x in enumerate(ordered(core, f)):
                perturb[k * FIELDS + f] = x.reshape(GROUPS, 8, LANES)
                turn_in(k * FIELDS + f, x)

    with jax.named_scope("deposit"):
        total[...] = jnp.zeros_like(total)
        per_list = CAP // LANES
        span = 2

        @pl.loop(0, tiles // span)
        def _(i):
            for n in range(span):
                for c in range(2):
                    at = (i * span + n) * 2 + c

                    @pl.when(at != core)
                    def _():
                        remote(
                            lists_out.at[0], lists_in.at[at], list_send.at[0, 0], list_recv.at[at], sibling, me_t
                        ).wait_recv()

            lists = lists_in[pl.ds(i * 2 * span, 2 * span)]
            cells = lists.astype(I32)
            channel = cells >> 15
            grid_row = (((channel & 1) ^ core) << 10) | ((channel >> 1) << 7) | (cells & (LON - 1))
            grid_lane = (cells >> 7) & (LAT - 1)
            grid_lane = ((grid_lane & (GROUPS - 1)) << 3) | (grid_lane >> 5)
            high, low = split(lists)
            left, right = [], []
            for u in range(2 * span):
                for j in range(per_list):
                    here = iota((FIELDS * LON, LANES), 0) == grid_row[u, 3 + j : 4 + j]
                    left.append(jnp.where(here, 1.0, 0.0).astype(BF16))
                    here = iota((LAT, LANES), 0) == grid_lane[u, 3 + j : 4 + j]
                    right.append(
                        jnp.concatenate(
                            [
                                jnp.where(here, high[u, j : j + 1], 0.0).astype(BF16),
                                jnp.where(here, low[u, j : j + 1], 0.0).astype(BF16),
                            ],
                            axis=0,
                        )
                    )
            total[...] += dot(jnp.concatenate(left, axis=1), jnp.concatenate(right, axis=1), NT)

        for h in range(HALVES):
            lanes = slice(h * LANES, (h + 1) * LANES)
            lows = slice(LAT + h * LANES, LAT + (h + 1) * LANES)
            partial[h] = total[:, lanes] + total[:, lows]

    def rows(c):
        return pl.ds(pl.multiple_of(c * PART, PART), PART)

    def part_copy(d):
        c = other_chip(d)
        return remote(
            partial.at[:, rows(c)], partial_in.at[chip], part_send.at[d], part_recv.at[d], 2 * c + core, me_t
        )

    @pl.loop(1, CHIPS)
    def _(d):
        part_copy(d).start()

    share_copy.wait_recv()
    with jax.named_scope("prepare"):
        faces = []
        for b in range(GROUPS):
            faces.append(coef_x_raw[pl.ds(b, 8, stride=GROUPS), :])
            face = coef_y_raw[pl.ds(b, 8, stride=GROUPS), :]
            if b == GROUPS - 1:
                face = jnp.where(iota((8, LANES), 0) < 7, face, 0.0)
            coef_y[b] = face
        faces = jnp.concatenate(faces, axis=0)
        for h in range(HALVES):
            coef_t[h, HALO : HALO + LON] = faces[h * LANES : (h + 1) * LANES].T
        for i in range(own, 2 * own):
            turn_in(i, perturb[i].reshape(LAT, LANES))

    def at_p(start):
        return perturb_t.at[:, :, pl.ds(start, HALO)]

    def at_c(start):
        return coef_t.at[:, pl.ds(start, HALO)]

    edge_copies = []
    for i, at in enumerate((at_p, at_c)):
        edge_copies.append(remote(at(LON), at(0), edge_send.at[i, 0], edge_recv.at[i, 0], me_m, east))
        edge_copies.append(
            remote(at(HALO), at(HALO + LON), edge_send.at[i, 1], edge_recv.at[i, 1], me_m, west)
        )
    for copy in edge_copies:
        copy.start()

    def block(c):
        start = pl.multiple_of(HALO + lax.rem(c, 4) * PART, 8)
        return adjoint_t.at[c // 4, :, pl.ds(start, PART)]

    def add_part(d, acc):
        part_copy(d).wait_recv()
        return acc + partial_in[other_chip(CHIPS - d)]

    block(chip)[...] = lax.fori_loop(1, CHIPS, add_part, partial[:, rows(chip)])

    def adj_copy(d):
        mine = block(chip)
        return remote(mine, mine, adj_send.at[d], adj_recv.at[chip], 2 * other_chip(d) + core, me_t)

    def adj_from(c):
        there = block(c)
        return remote(there, there, adj_send.at[0], adj_recv.at[c], 2 * other_chip(1) + core, me_t)

    def halo_at(f, start):
        return adjoint_t.at[f, :, pl.ds(start, HALO)]

    def halo_copy(c, side):
        f = chip // 4
        source = halo_at(f, HALO if side else LON)
        target = halo_at(f, HALO + LON if side else 0)
        return remote(
            source, target, halo_send.at[c], halo_recv.at[f, side], 2 * c + core, west if side else east
        )

    def halo_from(f, side):
        target = halo_at(f, HALO + LON if side else 0)
        return remote(target, target, halo_send.at[0], halo_recv.at[f, side], me_m, east)

    for side in (0, 1):

        @pl.when(lax.rem(chip, 4) == (0 if side else 3))
        def _():
            @pl.loop(0, CHIPS)
            def _(c):
                halo_copy(c, side).start()

    @pl.loop(1, CHIPS)
    def _(d):
        adj_copy(d).start()

    for copy in edge_copies:
        copy.wait_recv()

    with jax.named_scope("gather"):

        @pl.loop(0, 2 * own)
        def _(i):
            for h in range(HALVES):
                for b in range(STEPS):
                    perturb_g[i, h, b] = perturb_t[i, h, pl.ds(b, 8, stride=STEPS), :]

        for h in range(HALVES):
            for b in range(STEPS):
                coef_g[h, b] = coef_t[h, pl.ds(b, 8, stride=STEPS), :]

    @pl.loop(1, CHIPS)
    def _(d):
        adj_from(other_chip(d)).wait_recv()

    for f in range(FIELDS):
        for side in (0, 1):
            halo_from(f, side).wait_recv()

    with jax.named_scope("east"):
        for f in range(FIELDS):
            for h in range(HALVES):
                for b in range(STEPS):
                    adjoint_g[f, h, b] = adjoint_t[f, h, pl.ds(b, 8, stride=STEPS), :]

        for h in range(HALVES):

            @pl.loop(0, 2 * members)
            def _(k):
                i = k * FIELDS
                v = [
                    perturb_g[i, h, b] * adjoint_g[0, h, b] + perturb_g[i + 1, h, b] * adjoint_g[1, h, b]
                    for b in range(STEPS)
                ]
                for _ in range(SWEEPS):
                    following = v[1:] + [pltpu.roll(v[0], 7, 0)]
                    flux = [coef_g[h, b] * (following[b] - v[b]) for b in range(STEPS)]
                    before = [pltpu.roll(flux[-1], 1, 0)] + flux[:-1]
                    v = [v[b] + flux[b] - before[b] for b in range(STEPS)]
                for b in range(STEPS):
                    diffused[k, h, pl.ds(b, 8, stride=STEPS), :] = v[b]

    with jax.named_scope("turn"):

        @pl.loop(0, members)
        def _(pair):
            for u in range(2):
                k = pair * 2 + u
                for h in range(HALVES):
                    turned = diffused[k, h, HALO : HALO + LON].T
                    half = GROUPS // HALVES
                    product[k, h * half : (h + 1) * half] = turned.reshape(half, 8, LANES)

    with jax.named_scope("north"):

        @pl.loop(0, 2 * members)
        def _(k):
            v = [product[k, b] for b in range(GROUPS)]
            for _ in range(SWEEPS):
                following = v[1:] + [pltpu.roll(v[0], 7, 0)]
                flux = [coef_y[b] * (following[b] - v[b]) for b in range(GROUPS)]
                before = [pltpu.roll(flux[-1], 1, 0)] + flux[:-1]
                v = [v[b] + flux[b] - before[b] for b in range(GROUPS)]
            for b in range(GROUPS):
                product[k, b] = v[b]

    share = LAT // mems

    with jax.named_scope("increments"):

        @pl.loop(0, GROUPS)
        def _(b):
            weights = [product[k, b] for k in range(2 * members)]
            for f in range(FIELDS):
                parts = [weights[k] * perturb[k * FIELDS + f, b] for k in range(2 * members)]
                while len(parts) > 1:
                    parts = [sum(parts[i : i + 2][1:], parts[i]) for i in range(0, len(parts), 2)]
                at = lax.rem(b, share) * 2 + f
                terms[b // share, pl.ds(at, 8, stride=2 * share), :] = parts[0]

    def out_rows(c):
        return pl.ds(pl.multiple_of(c * 2 * share, 2 * share), 2 * share)

    def term_copy(d):
        m = other_m(d)
        return remote(
            terms.at[lax.rem(m, 2), out_rows(m // 2)], terms_in.at[me_m], term_send.at[d], term_recv.at[d], m, me_t
        )

    @pl.loop(1, mems)
    def _(d):
        term_copy(d).start()

    terms_in[me_m] = terms[core, out_rows(chip)]

    @pl.loop(1, mems)
    def _(d):
        term_copy(d).wait_recv()

    for l in range(LEVELS):
        acc = terms_in[l]
        for c in range(1, CHIPS):
            acc = acc + terms_in[2 * c + l]
        out_ref[pl.ds(l, 2 * share, stride=LEVELS), :] = acc * (1.0 / (mems * members - 1))

    for copy in [to_sibling, share_copy] + edge_copies:
        copy.wait_send()

    for n in range(1, tiles):
        for to in range(2):
            list_copy(n, to).wait_send()

    @pl.loop(1, CHIPS)
    def _(d):
        part_copy(d).wait_send()
        adj_copy(d).wait_send()

    @pl.loop(1, mems)
    def _(d):
        term_copy(d).wait_send()

    for side in (0, 1):

        @pl.when(lax.rem(chip, 4) == (0 if side else 3))
        def _():
            @pl.loop(0, CHIPS)
            def _(c):
                halo_copy(c, side).wait_send()


def on_device(perturb, coef_x, coef_y, obs_values, obs_tile, obs_cell):
    tiles = lax.axis_size("tile")
    members = perturb.shape[0]
    own = members * FIELDS
    mems = 2 * CHIPS
    share = LAT // mems
    dma = pltpu.SemaphoreType.DMA

    def rows(*shape):
        return pltpu.VMEM((*shape, LANES), F32)

    out = pl.pallas_call(
        functools.partial(kernel, tiles=tiles, members=members),
        out_shape=jax.ShapeDtypeStruct((share * FIELDS * LEVELS, LANES), F32),
        in_specs=[pl.BlockSpec(memory_space=pl.ANY)] * 3 + [pl.BlockSpec(memory_space=pltpu.VMEM)] * 3,
        out_specs=pl.BlockSpec(memory_space=pltpu.VMEM),
        scratch_shapes=[
            pltpu.VMEM((own, LEVELS, LAT, LON), BF16),
            rows(LAT),
            rows(LAT),
            rows(2 * own, GROUPS, 8),
            rows(own, GROUPS, 8),
            rows(2 * own, HALVES, WIDE),
            rows(2 * own, HALVES, STEPS, 8),
            rows(HALVES, WIDE),
            rows(HALVES, STEPS, 8),
            rows(GROUPS, 8),
            rows(tiles, 8),
            rows(2 * tiles, 8),
            pltpu.VMEM((FIELDS * LON, 2 * LAT), F32),
            rows(HALVES, FIELDS * LON),
            rows(CHIPS, HALVES, PART),
            rows(FIELDS, HALVES, WIDE),
            rows(FIELDS, HALVES, STEPS, 8),
            rows(2 * members, HALVES, WIDE),
            rows(2 * members, GROUPS, 8),
            rows(2, LAT),
            rows(mems, 2 * share),
            dma((4,)),
            dma((tiles, 2)), dma((2 * tiles,)),
            dma((1,)), dma((1,)),
            dma((2, 2)), dma((2, 2)),
            dma((CHIPS,)), dma((CHIPS,)),
            dma((CHIPS,)), dma((CHIPS,)),
            dma((CHIPS,)), dma((FIELDS, 2)),
            dma((mems,)), dma((mems,)),
        ],
        compiler_params=pltpu.CompilerParams(
            collective_id=0, has_side_effects=True, vmem_limit_bytes=56 * 2**20
        ),
    )(
        perturb.reshape(own, LEVELS, LAT, LON),
        coef_x,
        coef_y,
        obs_values.reshape(-1, LANES),
        obs_tile.reshape(-1, LANES),
        obs_cell.reshape(-1, LANES),
    )
    return out.reshape(share, FIELDS, LEVELS, LANES)


def solution(mesh):
    return jax.shard_map(
        on_device,
        mesh=mesh,
        in_specs=(
            P("mem", None, None, None, "tile"),
            P(None, None, "tile"),
            P(None, None, "tile"),
            P(("mem", "tile")),
            P(("mem", "tile"), None),
            P(("mem", "tile")),
        ),
        out_specs=P("mem", None, None, "tile"),
        check_vma=False,
    )
```

time: 437 us -> 48.1 us (0.11)
  waiting for transfers between devices: 264 us -> 0 us
  other arithmetic: 72.8 us -> 0 us
  local copies, waits for them, and re-layouts: 48.6 us -> 1.38 us
  Pallas kernels: 0 us -> 46.5 us
  blocking collectives: 20.4 us -> 0 us
  starting transfers between devices: 16.5 us -> 0 us
  between operations: 14.4 us -> 0.01 us
    unnamed x3 -> x0, waiting for transfers between devices: 122 us -> none
    psum x1 -> x0, waiting for transfers between devices: 119 us -> none  [on_device(): adjoint_field = lax.psum(deposit(incoming, total_cells), 'mem')]
    pallas_call x0 -> x1, Pallas kernels: none -> 46.5 us  [on_device(): pl.pallas_call(functools.partial(kernel, tiles=tiles, members=members), o...]
    scatter-add x1 -> x0, other arithmetic: 41.6 us -> none  [deposit(): return jnp.zeros((total_cells,), jnp.float32).at[cells].add(lists[0])]
    ppermute x12 -> x0, waiting for transfers between devices: 22.7 us -> none  [the longest x6 20.2 us: extended_2(): lax.ppermute(lax.slice_in_dim(block, block.shape[dim] - width, None, axis...]
    slice x18 -> x0, local copies, waits for them, and re-layouts: 22.2 us -> none  [the longest x11 11.4 us: extended_2(): lax.slice_in_dim(block, block.shape[dim] - width, None, axis=dim)]
    all_to_all x1 -> x0, blocking collectives: 20.4 us -> none  [on_device(): lax.all_to_all(outgoing, 'tile', split_axis=1, concat_axis=1, tiled=True)]
    ppermute x12 -> x0, starting transfers between devices: 16.5 us -> none  [the longest x6 8.7 us: extended_2(): lax.ppermute(lax.slice_in_dim(block, 0, width, axis=dim), axis, backward)]
  transfers between devices with their start and end apart: 14 -> 0, of which waited for: 12 -> 0; matrix products, arithmetic and copies ran while one was open for 2% -> 0% of each run, Pallas kernels for 0% -> 0%
where the time goes in v3:
time: 48.1 us; the launch traced here: 47.9 us
  Pallas kernels  46.5 us (97%)
  local copies, waits for them, and re-layouts  1.38 us (3%)
    pallas_call x1, Pallas kernels, on_device(): pl.pallas_call(functools.partial(kernel, tiles=tiles, members=members), o...  46.5 us
    unnamed x1, local copies, waits for them, and re-layouts  1.38 us

profile of v3, /device:TPU:1, one launch (start us, length us, event | category | flops | bytes accessed | tf_op | source)
XLA Modules:
  0.0 47.9 jit_solution(8878450667670451818)
XLA Ops:
  0.0 46.5 %shard_map.64 = f32[64,128]{1,0:T(8,128)} custom-call(bf16[10,2,256,128]{3,2,1,0:T(8,128)(2,1)} %bitcast.5, f32[2,256,128]{2,1,0:T(8,128)} %coef_x_hbm.1, f32[2,256,128]{2,1,0:T(8,128)} %coef_y_hbm.1, f32[16,128]{1,0:T(8,128)} %bitcast.7, s32[16,128]{1,0:T(8,128)} %bitcast.8, s32[16,128]{1,0:T(8,128)} %bitcast.9), custom_call_target="tpu_custom_call" | custom-call | tf_op jit(solution)/shard_map/pallas_call | solution.py:478
  46.5 1.4 %copy.8 = f32[16,2,2,128]{3,2,1,0:T(2,128)} copy(f32[16,2,2,128]{3,2,1,0:T(2,128)} %bitcast.6) | data formatting | bytes 65536

commit v4 on v3

--- a/solution.py
+++ b/solution.py
@@ -195,11 +195,43 @@
             for k, x in enumerate(ordered(core, f)):
                 perturb[k * FIELDS + f] = x.reshape(GROUPS, 8, LANES)
                 turn_in(k * FIELDS + f, x)
+        faces = []
+        for b in range(GROUPS):
+            faces.append(coef_x_raw[pl.ds(b, 8, stride=GROUPS), :])
+            face = coef_y_raw[pl.ds(b, 8, stride=GROUPS), :]
+            if b == GROUPS - 1:
+                face = jnp.where(iota((8, LANES), 0) < 7, face, 0.0)
+            coef_y[b] = face
+        faces = jnp.concatenate(faces, axis=0)
+        for h in range(HALVES):
+            coef_t[h, HALO : HALO + LON] = faces[h * LANES : (h + 1) * LANES].T
+
+    def edges_of(start):
+        mine, theirs = pl.ds(0, own), pl.ds(own, own)
+        at = pl.ds(start, HALO)
+        return coef_t.at[:, at], perturb_t.at[mine, :, at], perturb_t.at[theirs, :, at]
+
+    edge_copies = []
+    for i in range(3):
+        edge_copies.append(
+            remote(edges_of(LON)[i], edges_of(0)[i], edge_send.at[i, 0], edge_recv.at[i, 0], me_m, east)
+        )
+        edge_copies.append(
+            remote(edges_of(HALO)[i], edges_of(HALO + LON)[i], edge_send.at[i, 1], edge_recv.at[i, 1], me_m, west)
+        )
+    for copy in edge_copies[:4]:
+        copy.start()
 
     with jax.named_scope("deposit"):
         total[...] = jnp.zeros_like(total)
+        counting = (iota((LAT // 16, 16, LANES), 0) * 16 + iota((LAT // 16, 16, LANES), 1)).astype(F32).astype(BF16)
+        one, zero = jnp.ones((), BF16), jnp.zeros((), BF16)
+
+        def repeated(x):
+            return jnp.broadcast_to(x, (16, LANES)).astype(BF16)[None]
+
         per_list = CAP // LANES
-        span = 2
+        span = 4
 
         @pl.loop(0, tiles // span)
         def _(i):
@@ -223,14 +255,14 @@
             left, right = [], []
             for u in range(2 * span):
                 for j in range(per_list):
-                    here = iota((FIELDS * LON, LANES), 0) == grid_row[u, 3 + j : 4 + j]
-                    left.append(jnp.where(here, 1.0, 0.0).astype(BF16))
-                    here = iota((LAT, LANES), 0) == grid_lane[u, 3 + j : 4 + j]
-                    right.append(
+                    here = counting == repeated(grid_lane.astype(F32)[u, 3 + j : 4 + j])
+                    right.append(jnp.where(here, one, zero).reshape(LAT, LANES))
+                    here = counting == repeated(grid_row.astype(F32)[u, 3 + j : 4 + j])
+                    left.append(
                         jnp.concatenate(
                             [
-                                jnp.where(here, high[u, j : j + 1], 0.0).astype(BF16),
-                                jnp.where(here, low[u, j : j + 1], 0.0).astype(BF16),
+                                jnp.where(here, repeated(part[u, j : j + 1]), zero).reshape(LAT, LANES)
+                                for part in (high, low)
                             ],
                             axis=0,
                         )
@@ -239,8 +271,7 @@
 
         for h in range(HALVES):
             lanes = slice(h * LANES, (h + 1) * LANES)
-            lows = slice(LAT + h * LANES, LAT + (h + 1) * LANES)
-            partial[h] = total[:, lanes] + total[:, lows]
+            partial[h] = total[: FIELDS * LON, lanes] + total[FIELDS * LON :, lanes]
 
     def rows(c):
         return pl.ds(pl.multiple_of(c * PART, PART), PART)
@@ -257,32 +288,10 @@
 
     share_copy.wait_recv()
     with jax.named_scope("prepare"):
-        faces = []
-        for b in range(GROUPS):
-            faces.append(coef_x_raw[pl.ds(b, 8, stride=GROUPS), :])
-            face = coef_y_raw[pl.ds(b, 8, stride=GROUPS), :]
-            if b == GROUPS - 1:
-                face = jnp.where(iota((8, LANES), 0) < 7, face, 0.0)
-            coef_y[b] = face
-        faces = jnp.concatenate(faces, axis=0)
-        for h in range(HALVES):
-            coef_t[h, HALO : HALO + LON] = faces[h * LANES : (h + 1) * LANES].T
         for i in range(own, 2 * own):
             turn_in(i, perturb[i].reshape(LAT, LANES))
 
-    def at_p(start):
-        return perturb_t.at[:, :, pl.ds(start, HALO)]
-
-    def at_c(start):
-        return coef_t.at[:, pl.ds(start, HALO)]
-
-    edge_copies = []
-    for i, at in enumerate((at_p, at_c)):
-        edge_copies.append(remote(at(LON), at(0), edge_send.at[i, 0], edge_recv.at[i, 0], me_m, east))
-        edge_copies.append(
-            remote(at(HALO), at(HALO + LON), edge_send.at[i, 1], edge_recv.at[i, 1], me_m, west)
-        )
-    for copy in edge_copies:
+    for copy in edge_copies[4:]:
         copy.start()
 
     def block(c):
@@ -359,33 +368,38 @@
                 for b in range(STEPS):
                     adjoint_g[f, h, b] = adjoint_t[f, h, pl.ds(b, 8, stride=STEPS), :]
 
-        for h in range(HALVES):
-
-            @pl.loop(0, 2 * members)
-            def _(k):
-                i = k * FIELDS
-                v = [
-                    perturb_g[i, h, b] * adjoint_g[0, h, b] + perturb_g[i + 1, h, b] * adjoint_g[1, h, b]
-                    for b in range(STEPS)
-                ]
-                for _ in range(SWEEPS):
-                    following = v[1:] + [pltpu.roll(v[0], 7, 0)]
-                    flux = [coef_g[h, b] * (following[b] - v[b]) for b in range(STEPS)]
-                    before = [pltpu.roll(flux[-1], 1, 0)] + flux[:-1]
-                    v = [v[b] + flux[b] - before[b] for b in range(STEPS)]
-                for b in range(STEPS):
-                    diffused[k, h, pl.ds(b, 8, stride=STEPS), :] = v[b]
+        @pl.loop(0, 2 * members)
+        def _(k):
+            i = k * FIELDS
+            places = [(h, b) for h in range(HALVES) for b in range(STEPS)]
+            v = {
+                p: perturb_g[i, *p] * adjoint_g[0, *p] + perturb_g[i + 1, *p] * adjoint_g[1, *p]
+                for p in places
+            }
+            for _ in range(SWEEPS):
+                end = [pltpu.roll(v[h, 0], 7, 0) for h in range(HALVES)]
+                flux = {
+                    (h, b): coef_g[h, b] * ((v[h, b + 1] if b + 1 < STEPS else end[h]) - v[h, b])
+                    for h, b in places
+                }
+                start = [pltpu.roll(flux[h, STEPS - 1], 1, 0) for h in range(HALVES)]
+                v = {
+                    (h, b): v[h, b] + flux[h, b] - (flux[h, b - 1] if b else start[h])
+                    for h, b in places
+                }
+            for h, b in places:
+                diffused[k, h, pl.ds(b, 8, stride=STEPS), :] = v[h, b]
 
     with jax.named_scope("turn"):
-
-        @pl.loop(0, members)
-        def _(pair):
+        twice = jnp.where((iota((LAT, 2 * LAT), 1) & (LAT - 1)) == iota((LAT, 2 * LAT), 0), 1.0, 0.0).astype(BF16)
+        for pair in range(members):
+            sides = []
+            for k in (2 * pair, 2 * pair + 1):
+                parts = [split(diffused[k, h, HALO : HALO + LON]) for h in range(HALVES)]
+                sides.append(jnp.concatenate([p[i] for i in range(2) for p in parts], axis=1).astype(BF16))
+            turned = dot(twice, jnp.concatenate(sides, axis=0), NT)
             for u in range(2):
-                k = pair * 2 + u
-                for h in range(HALVES):
-                    turned = diffused[k, h, HALO : HALO + LON].T
-                    half = GROUPS // HALVES
-                    product[k, h * half : (h + 1) * half] = turned.reshape(half, 8, LANES)
+                product[2 * pair + u] = turned[:, u * LON : (u + 1) * LON].reshape(GROUPS, 8, LANES)
 
     with jax.named_scope("north"):
 
@@ -402,36 +416,46 @@
 
     share = LAT // mems
 
-    with jax.named_scope("increments"):
-
-        @pl.loop(0, GROUPS)
+    def out_rows(c):
+        return pl.ds(pl.multiple_of(c * 2 * share, 2 * share), 2 * share)
+
+    def term_copy(to, d):
+        c = other_chip(d)
+        return remote(
+            terms.at[to, out_rows(c)], terms_in.at[me_m], term_send.at[to, c], term_recv.at[me_m], 2 * c + to, me_t
+        )
+
+    def increments(half):
+        @pl.loop(0, share, unroll=4)
         def _(b):
-            weights = [product[k, b] for k in range(2 * members)]
+            at = half * share + b
+            weights = [product[k, at] for k in range(2 * members)]
             for f in range(FIELDS):
-                parts = [weights[k] * perturb[k * FIELDS + f, b] for k in range(2 * members)]
+                parts = [weights[k] * perturb[k * FIELDS + f, at] for k in range(2 * members)]
                 while len(parts) > 1:
                     parts = [sum(parts[i : i + 2][1:], parts[i]) for i in range(0, len(parts), 2)]
-                at = lax.rem(b, share) * 2 + f
-                terms[b // share, pl.ds(at, 8, stride=2 * share), :] = parts[0]
-
-    def out_rows(c):
-        return pl.ds(pl.multiple_of(c * 2 * share, 2 * share), 2 * share)
-
-    def term_copy(d):
+                terms[half, pl.ds(2 * b + f, 8, stride=2 * share), :] = parts[0]
+
+    with jax.named_scope("increments"):
+        increments(1 - core)
+
+    @pl.loop(0, CHIPS)
+    def _(d):
+        term_copy(1 - core, d).start()
+
+    with jax.named_scope("increments"):
+        increments(core)
+
+    @pl.loop(1, CHIPS)
+    def _(d):
+        term_copy(core, d).start()
+
+    terms_in[me_m] = terms[core, out_rows(chip)]
+
+    @pl.loop(1, mems)
+    def _(d):
         m = other_m(d)
-        return remote(
-            terms.at[lax.rem(m, 2), out_rows(m // 2)], terms_in.at[me_m], term_send.at[d], term_recv.at[d], m, me_t
-        )
-
-    @pl.loop(1, mems)
-    def _(d):
-        term_copy(d).start()
-
-    terms_in[me_m] = terms[core, out_rows(chip)]
-
-    @pl.loop(1, mems)
-    def _(d):
-        term_copy(d).wait_recv()
+        remote(terms_in.at[m], terms_in.at[m], term_send.at[0, 0], term_recv.at[m], sibling, me_t).wait_recv()
 
     for l in range(LEVELS):
         acc = terms_in[l]
@@ -450,10 +474,11 @@
     def _(d):
         part_copy(d).wait_send()
         adj_copy(d).wait_send()
-
-    @pl.loop(1, mems)
-    def _(d):
-        term_copy(d).wait_send()
+        term_copy(core, d).wait_send()
+
+    @pl.loop(0, CHIPS)
+    def _(d):
+        term_copy(1 - core, d).wait_send()
 
     for side in (0, 1):
 
@@ -493,7 +518,7 @@
             rows(GROUPS, 8),
             rows(tiles, 8),
             rows(2 * tiles, 8),
-            pltpu.VMEM((FIELDS * LON, 2 * LAT), F32),
+            pltpu.VMEM((2 * FIELDS * LON, LAT), F32),
             rows(HALVES, FIELDS * LON),
             rows(CHIPS, HALVES, PART),
             rows(FIELDS, HALVES, WIDE),
@@ -505,11 +530,11 @@
             dma((4,)),
             dma((tiles, 2)), dma((2 * tiles,)),
             dma((1,)), dma((1,)),
-            dma((2, 2)), dma((2, 2)),
+            dma((3, 2)), dma((3, 2)),
             dma((CHIPS,)), dma((CHIPS,)),
             dma((CHIPS,)), dma((CHIPS,)),
             dma((CHIPS,)), dma((FIELDS, 2)),
-            dma((mems,)), dma((mems,)),
+            dma((2, CHIPS)), dma((mems,)),
         ],
         compiler_params=pltpu.CompilerParams(
             collective_id=0, has_side_effects=True, vmem_limit_bytes=56 * 2**20

time: 48.1 us -> 46 us (0.956)
  Pallas kernels: 46.5 us -> 44.5 us
    pallas_call x1, Pallas kernels: 46.5 us -> 44.5 us  [on_device(): pl.pallas_call(functools.partial(kernel, tiles=tiles, members=members), o...]
where the time goes in v4:
time: 46 us; the launch traced here: 45.9 us
  Pallas kernels  44.5 us (97%)
  local copies, waits for them, and re-layouts  1.38 us (3%)
    pallas_call x1, Pallas kernels, on_device(): pl.pallas_call(functools.partial(kernel, tiles=tiles, members=members), o...  44.5 us
    unnamed x1, local copies, waits for them, and re-layouts  1.38 us

profile of v4, /device:TPU:1, one launch (start us, length us, event | category | flops | bytes accessed | tf_op | source)
XLA Modules:
  0.0 45.9 jit_solution(3287598711131335841)
XLA Ops:
  0.0 44.5 %shard_map.64 = f32[64,128]{1,0:T(8,128)} custom-call(bf16[10,2,256,128]{3,2,1,0:T(8,128)(2,1)} %bitcast.5, f32[2,256,128]{2,1,0:T(8,128)} %coef_x_hbm.1, f32[2,256,128]{2,1,0:T(8,128)} %coef_y_hbm.1, f32[16,128]{1,0:T(8,128)} %bitcast.7, s32[16,128]{1,0:T(8,128)} %bitcast.8, s32[16,128]{1,0:T(8,128)} %bitcast.9), custom_call_target="tpu_custom_call" | custom-call | tf_op jit(solution)/shard_map/pallas_call | solution.py:503
  44.5 1.4 %copy.8 = f32[16,2,2,128]{3,2,1,0:T(2,128)} copy(f32[16,2,2,128]{3,2,1,0:T(2,128)} %bitcast.6) | data formatting | bytes 65536

commit v5 on v4

--- a/solution.py
+++ b/solution.py
@@ -72,6 +72,8 @@
 
     def other_chip(d):
         return lax.rem(chip + d, CHIPS)
+
+    order7 = [lax.rem(chip // 4 + y, 2) * 4 + lax.rem(lax.rem(chip, 4) + x, 4) for y, x in ((1, 2), (1, 1), (1, 3), (0, 2), (1, 0), (0, 1), (0, 3))]
 
     def other_m(d):
         return lax.rem(me_m + d, mems)
@@ -222,6 +224,14 @@
     for copy in edge_copies[:4]:
         copy.start()
 
+    share_copy.wait_recv()
+    with jax.named_scope("prepare"):
+        for i in range(own, 2 * own):
+            turn_in(i, perturb[i].reshape(LAT, LANES))
+
+    for copy in edge_copies[4:]:
+        copy.start()
+
     with jax.named_scope("deposit"):
         total[...] = jnp.zeros_like(total)
         counting = (iota((LAT // 16, 16, LANES), 0) * 16 + iota((LAT // 16, 16, LANES), 1)).astype(F32).astype(BF16)
@@ -282,17 +292,8 @@
             partial.at[:, rows(c)], partial_in.at[chip], part_send.at[d], part_recv.at[d], 2 * c + core, me_t
         )
 
-    @pl.loop(1, CHIPS)
-    def _(d):
-        part_copy(d).start()
-
-    share_copy.wait_recv()
-    with jax.named_scope("prepare"):
-        for i in range(own, 2 * own):
-            turn_in(i, perturb[i].reshape(LAT, LANES))
-
-    for copy in edge_copies[4:]:
-        copy.start()
+    for c in order7:
+        part_copy(lax.rem(c - chip + CHIPS, CHIPS)).start()
 
     def block(c):
         start = pl.multiple_of(HALO + lax.rem(c, 4) * PART, 8)
@@ -335,9 +336,8 @@
             def _(c):
                 halo_copy(c, side).start()
 
-    @pl.loop(1, CHIPS)
-    def _(d):
-        adj_copy(d).start()
+    for c in order7:
+        adj_copy(lax.rem(c - chip + CHIPS, CHIPS)).start()
 
     for copy in edge_copies:
         copy.wait_recv()
@@ -439,16 +439,14 @@
     with jax.named_scope("increments"):
         increments(1 - core)
 
-    @pl.loop(0, CHIPS)
-    def _(d):
-        term_copy(1 - core, d).start()
+    for c in order7 + [chip]:
+        term_copy(1 - core, lax.rem(c - chip + CHIPS, CHIPS)).start()
 
     with jax.named_scope("increments"):
         increments(core)
 
-    @pl.loop(1, CHIPS)
-    def _(d):
-        term_copy(core, d).start()
+    for c in order7:
+        term_copy(core, lax.rem(c - chip + CHIPS, CHIPS)).start()
 
     terms_in[me_m] = terms[core, out_rows(chip)]
 

time: 46 us -> 44.1 us (0.959)
  Pallas kernels: 44.5 us -> 42.5 us
    pallas_call x1, Pallas kernels: 44.5 us -> 42.5 us  [on_device(): pl.pallas_call(functools.partial(kernel, tiles=tiles, members=members), o...]
where the time goes in v5:
time: 44.1 us; the launch traced here: 43.9 us
  Pallas kernels  42.5 us (96%)
  local copies, waits for them, and re-layouts  1.38 us (3%)
    pallas_call x1, Pallas kernels, on_device(): pl.pallas_call(functools.partial(kernel, tiles=tiles, members=members), o...  42.5 us
    unnamed x1, local copies, waits for them, and re-layouts  1.38 us

profile of v5, /device:TPU:1, one launch (start us, length us, event | category | flops | bytes accessed | tf_op | source)
XLA Modules:
  0.0 43.9 jit_solution(13479635782722237291)
XLA Ops:
  0.0 42.5 %shard_map.64 = f32[64,128]{1,0:T(8,128)} custom-call(bf16[10,2,256,128]{3,2,1,0:T(8,128)(2,1)} %bitcast.5, f32[2,256,128]{2,1,0:T(8,128)} %coef_x_hbm.1, f32[2,256,128]{2,1,0:T(8,128)} %coef_y_hbm.1, f32[16,128]{1,0:T(8,128)} %bitcast.7, s32[16,128]{1,0:T(8,128)} %bitcast.8, s32[16,128]{1,0:T(8,128)} %bitcast.9), custom_call_target="tpu_custom_call" | custom-call | tf_op jit(solution)/shard_map/pallas_call | solution.py:501
  42.5 1.4 %copy.8 = f32[16,2,2,128]{3,2,1,0:T(2,128)} copy(f32[16,2,2,128]{3,2,1,0:T(2,128)} %bitcast.6) | data formatting | bytes 65536

commit v6 on v5

--- a/solution.py
+++ b/solution.py
@@ -44,7 +44,8 @@
 
 
 def kernel(
-    perturb_hbm, coef_x_hbm, coef_y_hbm, values_ref, tile_ref, cell_ref, out_ref,
+    perturb_hbm, coef_x_hbm, coef_y_hbm, values_hbm, tile_hbm, cell_hbm, out_ref,
+    values_ref, tile_ref, cell_ref,
     perturb_raw, coef_x_raw, coef_y_raw, perturb, perturb_out, perturb_t, perturb_g, coef_t, coef_g, coef_y,
     lists_out, lists_in, total, partial, partial_in, adjoint_t, adjoint_g, diffused, product, terms, terms_in,
     load_sem, list_send, list_recv, share_send, share_recv, edge_send, edge_recv, part_send, part_recv,
@@ -86,11 +87,12 @@
                 (perturb_hbm.at[:, core], perturb_raw.at[:, core]),
                 (coef_x_hbm.at[core], coef_x_raw),
                 (coef_y_hbm.at[core], coef_y_raw),
+                (tile_hbm, tile_ref),
+                (values_hbm, values_ref),
+                (cell_hbm, cell_ref),
             )
         )
     ]
-    for copy in loads:
-        copy.start()
 
     barrier = pltpu.get_barrier_semaphore()
     signal(sibling, me_t)
@@ -108,6 +110,11 @@
         signal(2 * other_chip(d) + 1 - core, me_t)
         signal(m, west)
         signal(m, east)
+
+    for copy in loads[4:] + loads[:4]:
+        copy.start()
+    for copy in loads[4:]:
+        copy.wait()
 
     with jax.named_scope("bucket"):
         tile = tile_ref[...]
@@ -190,7 +197,7 @@
             for k, x in enumerate(ordered(1 - core, f)):
                 perturb_out[k * FIELDS + f] = x.reshape(GROUPS, 8, LANES)
     share_copy.start()
-    for copy in loads[1:]:
+    for copy in loads[1:4]:
         copy.wait()
     with jax.named_scope("prepare"):
         for f in range(FIELDS):
@@ -232,68 +239,74 @@
     for copy in edge_copies[4:]:
         copy.start()
 
+    def rows(c):
+        return pl.ds(pl.multiple_of(c * PART, PART), PART)
+
+    def part_copy(d):
+        c = other_chip(d)
+        return remote(
+            partial.at[:, rows(c)], partial_in.at[chip], part_send.at[d], part_recv.at[d], 2 * c + core, me_t
+        )
+
     with jax.named_scope("deposit"):
-        total[...] = jnp.zeros_like(total)
+        per_list = CAP // LANES
+        span = 8
         counting = (iota((LAT // 16, 16, LANES), 0) * 16 + iota((LAT // 16, 16, LANES), 1)).astype(F32).astype(BF16)
         one, zero = jnp.ones((), BF16), jnp.zeros((), BF16)
 
         def repeated(x):
             return jnp.broadcast_to(x, (16, LANES)).astype(BF16)[None]
 
-        per_list = CAP // LANES
-        span = 4
-
-        @pl.loop(0, tiles // span)
-        def _(i):
-            for n in range(span):
-                for c in range(2):
-                    at = (i * span + n) * 2 + c
-
-                    @pl.when(at != core)
+        @pl.loop(0, FIELDS)
+        def _(turn):
+            f = lax.rem(1 - chip // 4 + turn, 2)
+            total[...] = jnp.zeros_like(total)
+
+            @pl.loop(0, tiles // span)
+            def _(i):
+                for n in range(2 * span):
+                    at = i * 2 * span + n
+
+                    @pl.when((turn == 0) & (at != core))
                     def _():
                         remote(
                             lists_out.at[0], lists_in.at[at], list_send.at[0, 0], list_recv.at[at], sibling, me_t
                         ).wait_recv()
 
-            lists = lists_in[pl.ds(i * 2 * span, 2 * span)]
-            cells = lists.astype(I32)
-            channel = cells >> 15
-            grid_row = (((channel & 1) ^ core) << 10) | ((channel >> 1) << 7) | (cells & (LON - 1))
-            grid_lane = (cells >> 7) & (LAT - 1)
-            grid_lane = ((grid_lane & (GROUPS - 1)) << 3) | (grid_lane >> 5)
-            high, low = split(lists)
-            left, right = [], []
-            for u in range(2 * span):
-                for j in range(per_list):
-                    here = counting == repeated(grid_lane.astype(F32)[u, 3 + j : 4 + j])
-                    right.append(jnp.where(here, one, zero).reshape(LAT, LANES))
-                    here = counting == repeated(grid_row.astype(F32)[u, 3 + j : 4 + j])
-                    left.append(
-                        jnp.concatenate(
-                            [
-                                jnp.where(here, repeated(part[u, j : j + 1]), zero).reshape(LAT, LANES)
-                                for part in (high, low)
-                            ],
-                            axis=0,
+                lists = lists_in[pl.ds(i * 2 * span, 2 * span)]
+                cells = lists.astype(I32)
+                channel = cells >> 15
+                grid_row = (((channel & 1) ^ core) << 10) | ((channel >> 1) << 7) | (cells & (LON - 1))
+                grid_row = (grid_row - f * LON).astype(F32)
+                grid_lane = (cells >> 7) & (LAT - 1)
+                grid_lane = (((grid_lane & (GROUPS - 1)) << 3) | (grid_lane >> 5)).astype(F32)
+                parts = split(lists)
+                left, right = [], []
+                for u in range(2 * span):
+                    for j in range(per_list):
+                        here = counting == repeated(grid_lane[u, 3 + j : 4 + j])
+                        right.append(jnp.where(here, one, zero).reshape(LAT, LANES))
+                        here = counting[: LON // 16] == repeated(grid_row[u, 3 + j : 4 + j])
+                        left.append(
+                            jnp.concatenate(
+                                [
+                                    jnp.where(here, repeated(part[u, j : j + 1]), zero).reshape(LON, LANES)
+                                    for part in parts
+                                ],
+                                axis=0,
+                            )
                         )
-                    )
-            total[...] += dot(jnp.concatenate(left, axis=1), jnp.concatenate(right, axis=1), NT)
-
-        for h in range(HALVES):
-            lanes = slice(h * LANES, (h + 1) * LANES)
-            partial[h] = total[: FIELDS * LON, lanes] + total[FIELDS * LON :, lanes]
-
-    def rows(c):
-        return pl.ds(pl.multiple_of(c * PART, PART), PART)
-
-    def part_copy(d):
-        c = other_chip(d)
-        return remote(
-            partial.at[:, rows(c)], partial_in.at[chip], part_send.at[d], part_recv.at[d], 2 * c + core, me_t
-        )
-
-    for c in order7:
-        part_copy(lax.rem(c - chip + CHIPS, CHIPS)).start()
+                total[...] += dot(jnp.concatenate(left, axis=1), jnp.concatenate(right, axis=1), NT)
+
+            for h in range(HALVES):
+                lanes = slice(h * LANES, (h + 1) * LANES)
+                partial[h, pl.ds(pl.multiple_of(f * LON, LON), LON)] = total[:LON, lanes] + total[LON:, lanes]
+            for x in (2, 1, 3, 0):
+                c = f * 4 + lax.rem(lax.rem(chip, 4) + x, 4)
+
+                @pl.when(c != chip)
+                def _():
+                    part_copy(lax.rem(c - chip + CHIPS, CHIPS)).start()
 
     def block(c):
         start = pl.multiple_of(HALO + lax.rem(c, 4) * PART, 8)
@@ -493,6 +506,7 @@
     own = members * FIELDS
     mems = 2 * CHIPS
     share = LAT // mems
+    blocks = obs_values.shape[0] // LANES
     dma = pltpu.SemaphoreType.DMA
 
     def rows(*shape):
@@ -501,9 +515,12 @@
     out = pl.pallas_call(
         functools.partial(kernel, tiles=tiles, members=members),
         out_shape=jax.ShapeDtypeStruct((share * FIELDS * LEVELS, LANES), F32),
-        in_specs=[pl.BlockSpec(memory_space=pl.ANY)] * 3 + [pl.BlockSpec(memory_space=pltpu.VMEM)] * 3,
+        in_specs=[pl.BlockSpec(memory_space=pl.ANY)] * 6,
         out_specs=pl.BlockSpec(memory_space=pltpu.VMEM),
         scratch_shapes=[
+            pltpu.VMEM((blocks, LANES), F32),
+            pltpu.VMEM((blocks, LANES), I32),
+            pltpu.VMEM((blocks, LANES), I32),
             pltpu.VMEM((own, LEVELS, LAT, LON), BF16),
             rows(LAT),
             rows(LAT),
@@ -516,7 +533,7 @@
             rows(GROUPS, 8),
             rows(tiles, 8),
             rows(2 * tiles, 8),
-            pltpu.VMEM((2 * FIELDS * LON, LAT), F32),
+            pltpu.VMEM((2 * LON, LAT), F32),
             rows(HALVES, FIELDS * LON),
             rows(CHIPS, HALVES, PART),
             rows(FIELDS, HALVES, WIDE),
@@ -525,7 +542,7 @@
             rows(2 * members, GROUPS, 8),
             rows(2, LAT),
             rows(mems, 2 * share),
-            dma((4,)),
+            dma((7,)),
             dma((tiles, 2)), dma((2 * tiles,)),
             dma((1,)), dma((1,)),
             dma((3, 2)), dma((3, 2)),

time: 44.1 us -> 42.1 us (0.955)
  Pallas kernels: 42.5 us -> 40.6 us
    pallas_call x1, Pallas kernels: 42.5 us -> 40.6 us  [on_device(): pl.pallas_call(functools.partial(kernel, tiles=tiles, members=members), o...]
where the time goes in v6:
time: 42.1 us; the launch traced here: 42 us
  Pallas kernels  40.6 us (96%)
  local copies, waits for them, and re-layouts  1.38 us (3%)
    pallas_call x1, Pallas kernels, on_device(): pl.pallas_call(functools.partial(kernel, tiles=tiles, members=members), o...  40.6 us
    unnamed x1, local copies, waits for them, and re-layouts  1.38 us

profile of v6, /device:TPU:1, one launch (start us, length us, event | category | flops | bytes accessed | tf_op | source)
XLA Modules:
  0.0 42.0 jit_solution(8016320420014879845)
XLA Ops:
  0.0 40.6 %shard_map.64 = f32[64,128]{1,0:T(8,128)} custom-call(bf16[10,2,256,128]{3,2,1,0:T(8,128)(2,1)} %bitcast.5, f32[2,256,128]{2,1,0:T(8,128)} %coef_x_hbm.1, f32[2,256,128]{2,1,0:T(8,128)} %coef_y_hbm.1, f32[16,128]{1,0:T(8,128)} %bitcast.7, s32[16,128]{1,0:T(8,128)} %bitcast.8, s32[16,128]{1,0:T(8,128)} %bitcast.9), custom_call_target="tpu_custom_call" | custom-call | tf_op jit(solution)/shard_map/pallas_call | solution.py:515
  40.6 1.4 %copy.8 = f32[16,2,2,128]{3,2,1,0:T(2,128)} copy(f32[16,2,2,128]{3,2,1,0:T(2,128)} %bitcast.6) | data formatting | bytes 65536
